TPU v7x, 512 devices: a whole 4x8x8 slice. The times are simulated.
512 devices in a mesh: ctx: 8 (over y_hi, core), exp: 64 (over x, z, y_lo).
Axes of the slice: x: 4, y: 8 (y_hi: 4, y_lo: 2; y = y_hi * 2 + y_lo), z: 8, core: 2. Of those that a mesh axis runs over, the one named last changes fastest.
Arguments:
- queries: bfloat16 [64, 512, 2048], P('exp', None, 'ctx'), may hold values from -6 to 6
- cache_kv: bfloat16 [64, 512, 512], P('exp', 'ctx'), may hold values from -12 to 12
- new_key_values: bfloat16 [64, 512, 512], P('exp', 'ctx'), may hold values from -12 to 12
- hidden: bfloat16 [64, 512, 2048], P('exp', 'ctx'), may hold values from -6 to 6
- out_weight: bfloat16 [2048, 2048], P('ctx'), may hold values from -0.25 to 0.25
- norm_gain: float32 [2048], replicated, may hold values from 0.1 to 1.9
- routes: int32 [64, 512, 8], P('exp', 'ctx'), may hold values from 0 to 63, all different within a row; in each aligned block of 64 rows (0 to 63, 64 to 127, ..., all dimensions but the last counted through in order) at most 10 rows name the same one
- gate_weights: float32 [64, 512, 8], P('exp', 'ctx'), may hold values from 0.05 to 0.3
- gate_up: bfloat16 [64, 2048, 768], P('exp', 'ctx'), may hold values from -0.125 to 0.125
- down_proj: bfloat16 [64, 2048, 384], P('exp', 'ctx'), may hold values from -0.3125 to 0.3125
Outputs:
- layer_out: bfloat16 [64, 512, 2048], P('exp', 'ctx')
Inputs may be any that keep to these rules, and one draw needn't show every extreme that they name: `routes`: each row names 8 different experts; of the 64 rows of one device (aligned blocks of rows, sequences and positions taken in order) at most 10 name the same expert.
All inputs are finite; a program needn't handle non-finite values.
Results may differ from a plain program's by a relative error of at most 0.017.
Values may be sent and summed in bfloat16 or wider, within the bound.
No kernel may reach another device: no remote copies, remote signals or barrier semaphores. Data moves between devices by JAX's collectives and lax.ppermute only.
A program may use at most 64 MiB of HBM per device.

v0:
```python
import jax
import jax.numpy as jnp
from jax import lax
from jax.sharding import PartitionSpec as P

QUERY_HEADS = 16
KEY_VALUE_HEADS = 2
HEAD_WIDTH = 128


norm_epsilon = 1e-06


def key_positions(row_index, block_rows, prefix_rows, own_rows):
    owner_dev = row_index // block_rows
    offset = row_index % block_rows
    return jnp.where(offset < prefix_rows, -1, owner_dev * own_rows + offset - prefix_rows)


def attend_keys(running, key_rows, value_row_block, key_pos, query_heads, span_index, score_scale):
    running_max, denominator, weighted = running
    scores = (
        jnp.einsum("hqd,kd->hqk", query_heads, key_rows, preferred_element_type=jnp.float32)
        * score_scale
    )
    visible = key_pos[None, None, :] <= span_index[None, :, None]
    block_max = jnp.max(jnp.where(visible, scores, -1e30), axis=2)
    new_max = jnp.maximum(running_max, block_max)
    weights = jnp.where(visible, jnp.exp(scores - new_max[:, :, None]), 0.0)
    denominator = jnp.sum(weights, axis=2)
    weighted = jnp.einsum(
        "hqk,kd->hqd",
        weights.astype(jnp.bfloat16),
        value_row_block,
        preferred_element_type=jnp.float32,
    )
    return (new_max, denominator, weighted)


def collect_weights(gate_up, down_proj):
    return (
        lax.all_gather(gate_up, "ctx", axis=1, tiled=True),
        lax.all_gather(down_proj, "ctx", axis=1, tiled=True),
    )


def on_device(
    queries,
    cache_kv,
    new_key_values,
    hidden,
    out_weight,
    norm_gain,
    routes,
    gate_weights,
    gate_up,
    down_proj,
):
    head_dimension = HEAD_WIDTH
    query_group_width = QUERY_HEADS // KEY_VALUE_HEADS
    local_heads = queries.shape[2] // head_dimension
    span_len = queries.shape[1]
    prefix_rows = cache_kv.shape[1]
    own_rows = new_key_values.shape[1]
    block_rows = prefix_rows + own_rows
    score_scale = head_dimension ** (-0.5)
    key_value_head = lax.axis_index("ctx") * local_heads // query_group_width
    query_heads = queries[0].reshape(span_len, local_heads, head_dimension).transpose(1, 0, 2)
    span_index = jnp.arange(span_len, dtype=jnp.int32)
    softmax_state = (
        jnp.full((local_heads, span_len), -1e30, jnp.float32),
        jnp.zeros((local_heads, span_len), jnp.float32),
        jnp.zeros((local_heads, span_len, head_dimension), jnp.float32),
    )
    kv_block = jnp.concatenate([cache_kv[0], new_key_values[0]], axis=0)
    key_value_slice = lax.all_gather(kv_block, "ctx", axis=0, tiled=True)
    row_index = jnp.arange(key_value_slice.shape[0], dtype=jnp.int32)
    key_rows = lax.dynamic_slice_in_dim(
        key_value_slice, key_value_head * head_dimension, head_dimension, 1
    )
    value_row_block = lax.dynamic_slice_in_dim(
        key_value_slice, (KEY_VALUE_HEADS + key_value_head) * head_dimension, head_dimension, 1
    )
    key_pos = key_positions(row_index, block_rows, prefix_rows, own_rows)
    softmax_state = attend_keys(
        softmax_state, key_rows, value_row_block, key_pos, query_heads, span_index, score_scale
    )
    heads_out = (softmax_state[2] / softmax_state[1][:, :, None]).astype(jnp.bfloat16)
    heads_out = heads_out.transpose(1, 0, 2).reshape(span_len, local_heads * head_dimension)
    head_mix = lax.psum_scatter(
        jnp.dot(heads_out, out_weight, preferred_element_type=jnp.float32).astype(jnp.bfloat16),
        "ctx",
        scatter_dimension=0,
        tiled=True,
    ).astype(jnp.float32)
    residual = hidden[0].astype(jnp.float32) + head_mix
    normed = (
        residual
        * lax.rsqrt(jnp.mean(residual * residual, axis=1, keepdims=True) + norm_epsilon)
        * norm_gain
    ).astype(jnp.bfloat16)
    fetched = collect_weights(gate_up, down_proj)
    experts = gate_up.shape[0] * lax.axis_size("exp")
    top_count = routes.shape[2]
    capacity = max(2, own_rows * top_count * 5 // (4 * experts))
    route_flat = routes[0].reshape(-1)
    onehot = (route_flat[:, None] == jnp.arange(experts, dtype=jnp.int32)[None, :]).astype(
        jnp.int32
    )
    slot_index = jnp.sum(onehot * (jnp.cumsum(onehot, axis=0) - 1), axis=1)
    slot_place = route_flat * capacity + slot_index
    selector = jnp.any(
        jnp.arange(experts * capacity, dtype=jnp.int32)[:, None, None]
        == slot_place.reshape(own_rows, top_count)[None, :, :],
        axis=2,
    ).astype(jnp.bfloat16)
    outgoing_rows = jnp.dot(selector, normed, preferred_element_type=jnp.float32).astype(
        jnp.bfloat16
    )
    outgoing_rows = outgoing_rows.reshape(experts, capacity, normed.shape[1])
    inner_width = fetched[1].shape[2]
    arrived = lax.all_to_all(outgoing_rows, "exp", split_axis=0, concat_axis=0, tiled=True)
    gathered = arrived.reshape(-1, arrived.shape[2])
    gate_and_up = jnp.dot(gathered, fetched[0][0], preferred_element_type=jnp.float32)
    activation = (jax.nn.silu(gate_and_up[:, :inner_width]) * gate_and_up[:, inner_width:]).astype(
        jnp.bfloat16
    )
    expert_out = lax.dot_general(
        activation, fetched[1][0], (((1,), (1,)), ((), ())), preferred_element_type=jnp.float32
    ).astype(jnp.bfloat16)
    results = lax.all_to_all(
        expert_out.reshape(arrived.shape), "exp", split_axis=0, concat_axis=0, tiled=True
    )
    picked = results.reshape(experts * capacity, -1)[slot_place].reshape(own_rows, top_count, -1)
    expert_sum = jnp.sum(picked.astype(jnp.float32) * gate_weights[0][:, :, None], axis=1)
    return (residual + expert_sum).astype(jnp.bfloat16)[None]


def solution(mesh):
    return jax.shard_map(
        on_device,
        mesh=mesh,
        in_specs=(
            P("exp", None, "ctx"),
            P("exp", "ctx", None),
            P("exp", "ctx", None),
            P("exp", "ctx", None),
            P("ctx", None),
            P(),
            P("exp", "ctx", None),
            P("exp", "ctx", None),
            P("exp", "ctx", None),
            P("exp", "ctx", None),
        ),
        out_specs=P("exp", "ctx", None),
        check_vma=False,
    )
```

profile of v0, /device:TPU:25, one launch (start us, length us, event | category | flops | bytes accessed | tf_op | source)
XLA Modules:
  0.0 370.1 jit_solution(9231265730126878395)
XLA Ops:
  6.5 0.0 copy-start
  6.5 0.0 all-gather.4.cloned.1.call-start
  6.5 1.6 pad_maximum_fusion
  8.2 0.0 all-gather.4.cloned.1.call-update
  8.2 0.0 reduce-scatter.2.cloned.1.call-start
  8.3 1.0 reshape_squeeze.4
  9.3 0.4 iota_compare_fusion
  9.7 34.9 %all-gather.4.cloned.1.call-done = bf16[1024,512]{1,0:T(8,128)(2,1)} async-done(((bf16[128,512]{1,0:T(8,128)(2,1)}), bf16[1024,512]{1,0:T(8,128)(2,1)}) %all-gather.4.cloned.1.call-update) | async-done | bytes 1048592 | tf_op jit(solution)/shard_map/all_gather | solution.py:76
  44.6 1.9 fusion.1
  46.5 1.0 fusion.4
  47.5 2.0 fusion.19
  49.5 0.0 copy-done
  49.5 0.0 copy-start.3
  49.5 0.0 copy-start.1
  49.5 2.1 convolution_convert_fusion.2
  51.6 0.0 copy-start.2
  51.6 0.0 reduce-scatter.2.cloned.1.call-update
  51.6 0.0 all-gather.6.cloned.1.call-start
  51.7 0.7 all-gather.6.cloned.1.call-update
  52.4 0.0 copy-done.3
  52.4 0.1 copy.27
  52.5 0.1 eq.47
  52.6 0.1 eq.43
  52.7 1.2 reduce-window.6
  53.9 0.2 slice_reduce_fusion
  54.1 0.1 fusion.37
  54.3 0.1 reduce_sum.42
  54.4 0.5 fusion.12
  54.9 42.4 %reduce-scatter.2.cloned.1.call-done = bf16[64,2048]{1,0:T(8,128)(2,1)} async-done(((bf16[512,2048]{1,0:T(8,128)(2,1)}), bf16[64,2048]{1,0:T(8,128)(2,1)}) %reduce-scatter.2.cloned.1.call-update) | async-done | bytes 262160 | tf_op jit(solution)/shard_map/reduce_scatter | solution.py:90
  97.2 0.0 copy-done.1
  97.2 1.1 multiply_reduce_fusion
  98.4 0.0 copy-done.2
  98.4 3.4 convolution_convert_fusion.1
  101.8 5.4 %reshape.133 = bf16[64,10,2048]{2,1,0:T(8,128)(2,1)} reshape(bf16[640,2048]{1,0:T(8,128)(2,1)} %convolution_convert_fusion.1) | data formatting | bytes 5242880 | tf_op jit(solution)/shard_map/reshape | solution.py:120
  107.2 13.4 %all-to-all-start = ((bf16[64,10,2048]{2,1,0:T(8,128)(2,1)}), bf16[64,10,2048]{2,1,0:T(8,128)(2,1)}, u32[]{:S(2)}, u32[]{:S(2)}) async-start(bf16[64,10,2048]{2,1,0:T(8,128)(2,1)} %reshape.133), calls=%async_computation.1 | async-start | bytes 8388608 | tf_op jit(solution)/shard_map/all_to_all | solution.py:122
  120.6 0.0 all-gather.8.cloned.1.call-start
  120.6 0.5 all-gather.8.cloned.1.call-update
  121.1 96.4 %all-to-all-done = bf16[64,10,2048]{2,1,0:T(8,128)(2,1)} async-done(((bf16[64,10,2048]{2,1,0:T(8,128)(2,1)}), bf16[64,10,2048]{2,1,0:T(8,128)(2,1)}, u32[]{:S(2)}, u32[]{:S(2)}) %all-to-all-start) | async-done | bytes 2621472 | tf_op jit(solution)/shard_map/all_to_all | solution.py:122
  217.6 5.5 %reshape.134 = bf16[640,2048]{1,0:T(8,128)(2,1)} reshape(bf16[64,10,2048]{2,1,0:T(8,128)(2,1)} %all-to-all-done) | data formatting | bytes 5242880 | tf_op jit(solution)/shard_map/reshape | solution.py:123
  223.1 0.0 all-gather.6.cloned.1.call-done
  223.1 6.2 %fusion.6 = f32[640,768]{1,0:T(8,128)} fusion(bf16[640,2048]{1,0:T(8,128)(2,1)} %reshape.134, bf16[1,2048,768]{2,1,0:T(8,128)(2,1)} %all-gather.6.cloned.1.call-done), kind=kOutput, calls=%fused_computation.12 | convolution fusion | flops 2013265920 | bytes 7733248 | tf_op jit(solution)/shard_map/dot_general | solution.py:124
  229.3 0.0 all-gather.8.cloned.1.call-done
  229.3 5.1 %convolution_convert_fusion = bf16[640,2048]{1,0:T(8,128)(2,1)} fusion(bf16[1,2048,384]{2,1,0:T(8,128)(2,1)} %all-gather.8.cloned.1.call-done, f32[640,768]{1,0:T(8,128)} %fusion.6), kind=kOutput, calls=%fused_computation.10 | convolution fusion | flops 1009418240 | bytes 6160384 | tf_op jit(solution)/shard_map/dot_general | solution.py:128
  234.4 5.4 %reshape.135 = bf16[64,10,2048]{2,1,0:T(8,128)(2,1)} reshape(bf16[640,2048]{1,0:T(8,128)(2,1)} %convolution_convert_fusion) | data formatting | bytes 5242880 | tf_op jit(solution)/shard_map/reshape | solution.py:132
  239.8 0.0 copy-start.4
  239.8 9.5 %all-to-all-start.1 = ((bf16[64,10,2048]{2,1,0:T(8,128)(2,1)}), bf16[64,10,2048]{2,1,0:T(8,128)(2,1)}, u32[]{:S(2)}, u32[]{:S(2)}) async-start(bf16[64,10,2048]{2,1,0:T(8,128)(2,1)} %reshape.135), calls=%async_computation.2 | async-start | bytes 8388608 | tf_op jit(solution)/shard_map/all_to_all | solution.py:131
  249.3 0.1 mul.100
  249.4 0.0 copy-done.4
  249.4 0.1 copy.31
  249.5 98.4 %all-to-all-done.1 = bf16[64,10,2048]{2,1,0:T(8,128)(2,1)} async-done(((bf16[64,10,2048]{2,1,0:T(8,128)(2,1)}), bf16[64,10,2048]{2,1,0:T(8,128)(2,1)}, u32[]{:S(2)}, u32[]{:S(2)}) %all-to-all-start.1) | async-done | bytes 2621472 | tf_op jit(solution)/shard_map/all_to_all | solution.py:131
  347.9 5.6 %reshape.136 = bf16[640,2048]{1,0:T(8,128)(2,1)} reshape(bf16[64,10,2048]{2,1,0:T(8,128)(2,1)} %all-to-all-done.1) | data formatting | bytes 5242880 | tf_op jit(solution)/shard_map/reshape | solution.py:134
  353.5 6.5 %gather_fusion = bf16[512,2048]{1,0:T(8,128)(2,1)S(1)} fusion(bf16[640,2048]{1,0:T(8,128)(2,1)} %reshape.136, s32[1024]{0:T(1024)S(1)} %pad_clamp_fusion), kind=kCustom, calls=%fused_computation | custom fusion | bytes 4196352 | tf_op jit(solution)/shard_map/gather | solution.py:134
  359.9 1.8 fusion
  361.8 1.8 fusion.25
  (9 shorter events, 0.1 us)
Async XLA Ops:
  6.5 42.9 %copy-start = (bf16[256,2048]{1,0:T(8,128)(2,1)S(1)}, bf16[256,2048]{1,0:T(8,128)(2,1)}, u32[]{:S(2)}) copy-start(bf16[256,2048]{1,0:T(8,128)(2,1)} %param.14) | copy-start | bytes 3145732
  6.5 38.0 %all-gather.4.cloned.1.call-start = ((), (), s32[]{:S(2)}) async-start(), calls=%async_computation.3 | async-start | bytes 1179648 | tf_op jit(solution)/shard_map/all_gather | solution.py:76
  8.2 89.0 %reduce-scatter.2.cloned.1.call-start = ((), (), s32[]{:S(2)}) async-start(), calls=%async_computation.4 | async-start | bytes 2359296 | tf_op jit(solution)/shard_map/reduce_scatter | solution.py:90
  49.5 2.9 copy-start.3
  49.5 47.7 %copy-start.1 = (bf16[1,64,2048]{2,1,0:T(8,128)(2,1)S(1)}, bf16[1,64,2048]{2,1,0:T(8,128)(2,1)}, u32[]{:S(2)}) copy-start(bf16[1,64,2048]{2,1,0:T(8,128)(2,1)} %param.13) | copy-start | bytes 786436
  51.6 46.8 %copy-start.2 = (f32[2048]{0:T(1024)S(1)}, f32[2048]{0:T(1024)}, u32[]{:S(2)}) copy-start(f32[2048]{0:T(1024)} %param.15) | copy-start | bytes 24580
  51.6 171.5 %all-gather.6.cloned.1.call-start = ((), (), s32[]{:S(2)}) async-start(), calls=%async_computation.5 | async-start | bytes 3538944 | tf_op jit(solution)/shard_map/all_gather | solution.py:42
  107.2 110.4 %all-to-all-start = ((bf16[64,10,2048]{2,1,0:T(8,128)(2,1)}), bf16[64,10,2048]{2,1,0:T(8,128)(2,1)}, u32[]{:S(2)}, u32[]{:S(2)}) async-start(bf16[64,10,2048]{2,1,0:T(8,128)(2,1)} %reshape.133), calls=%async_computation.1 | async-start | bytes 8388608 | tf_op jit(solution)/shard_map/all_to_all | solution.py:122
  120.6 108.8 %all-gather.8.cloned.1.call-start = ((), (), s32[]{:S(2)}) async-start(), calls=%async_computation.6 | async-start | bytes 1769472 | tf_op jit(solution)/shard_map/all_gather | solution.py:43
  239.8 9.6 %copy-start.4 = (f32[1,64,8]{1,2,0:T(8,128)S(1)}, f32[1,64,8]{1,2,0:T(8,128)}, u32[]{:S(2)}) copy-start(f32[1,64,8]{1,2,0:T(8,128)} %param.17) | copy-start | bytes 6148
  239.8 108.1 %all-to-all-start.1 = ((bf16[64,10,2048]{2,1,0:T(8,128)(2,1)}), bf16[64,10,2048]{2,1,0:T(8,128)(2,1)}, u32[]{:S(2)}, u32[]{:S(2)}) async-start(bf16[64,10,2048]{2,1,0:T(8,128)(2,1)} %reshape.135), calls=%async_computation.2 | async-start | bytes 8388608 | tf_op jit(solution)/shard_map/all_to_all | solution.py:131
Sparse Core Ops, SparseCore 0:
  9.5 35.0 all-gather.3
  51.8 45.4 reduce-scatter.1
  99.4 59.9 all-gather.5
  161.3 38.7 all-gather.7
where the time goes:
time: 371 us; the launch traced here: 370 us
  waiting for transfers between devices  273 us (74%)
  local copies, waits for them, and re-layouts  30.1 us (8%)
  starting transfers between devices  23 us (6%)
  matrix products  20.7 us (6%)
  between operations  13.3 us (4%)
  other arithmetic  9.56 us (3%)
    all_to_all x1, waiting for transfers between devices, on_device(): lax.all_to_all(expert_out.reshape(arrived.shape), 'exp', split_axis=0, co...  98.4 us
    all_to_all x1, waiting for transfers between devices, on_device(): lax.all_to_all(outgoing_rows, 'exp', split_axis=0, concat_axis=0, tiled=T...  96.4 us
    reduce_scatter x1, waiting for transfers between devices, on_device(): lax.psum_scatter(jnp.dot(heads_out, out_weight, preferred_element_type=jn...  42.4 us
    all_gather x1, waiting for transfers between devices, on_device(): key_value_slice = lax.all_gather(kv_block, 'ctx', axis=0, tiled=True)  34.9 us
    all_to_all x1, starting transfers between devices, on_device(): lax.all_to_all(outgoing_rows, 'exp', split_axis=0, concat_axis=0, tiled=T...  13.4 us
    all_to_all x1, starting transfers between devices, on_device(): lax.all_to_all(expert_out.reshape(arrived.shape), 'exp', split_axis=0, co...  9.48 us
  transfers between devices with their start and end apart: 6, of which 4 were waited for; matrix products, arithmetic and copies ran while one was open for 7% of the time, Pallas kernels for 0%

commit v1 on v0

v1 whole, which is shorter than its diff:
```python
import jax
import jax.numpy as jnp
from jax import lax
from jax.experimental import pallas as pl
from jax.experimental.pallas import tpu as pltpu
from jax.sharding import Mesh
from jax.sharding import PartitionSpec as P

D = 2048
HEAD_WIDTH = 128
FF = 384
TOK = 64
EXPERTS = 64
CAP = 10
KEYS = 1024
PARTS = 4
WIDTH = D // PARTS
BLOCK = PARTS * CAP
ROWS = EXPERTS * BLOCK
LANES = PARTS * TOK
GROUP = 4
NORM_EPSILON = 1e-06
MIB = 1 << 20

CTX = ("yh", "core")
EXP = ("x", "z", "yl")


def whole(count):
    return [pl.BlockSpec(memory_space=pltpu.VMEM)] * count


def f32_dot(a, b):
    return jnp.dot(a, b, preferred_element_type=jnp.float32)


def iota(shape, dim):
    return lax.broadcasted_iota(jnp.int32, shape, dim)


def attend_kernel(core_ref, q_own, q_other, kv, w_own, w_other, out, heads):
    base = core_ref[0] * TOK
    key_index = iota((4 * TOK, KEYS), 1)
    within = key_index & 127
    key_pos = jnp.where(within < TOK, -1, ((key_index >> 7) * TOK) + within - TOK)
    row_pos = (iota((4 * TOK, KEYS), 0) & (TOK - 1)) + base
    keys = kv[:, :HEAD_WIDTH]
    values = kv[:, HEAD_WIDTH:]
    for block in range(4):
        rows = slice(block * TOK, (block + 1) * TOK)
        q = jnp.concatenate(
            [ref[rows, h * HEAD_WIDTH : (h + 1) * HEAD_WIDTH] for ref in (q_own, q_other) for h in range(2)],
            axis=0,
        )
        scores = lax.dot_general(q, keys, (((1,), (1,)), ((), ())), preferred_element_type=jnp.float32)
        scores = scores * (HEAD_WIDTH**-0.5)
        scores = jnp.where(key_pos <= row_pos + block * 2 * TOK, scores, -1e30)
        peak = jnp.max(scores, axis=1, keepdims=True)
        probs = jnp.exp(scores - peak)
        denom = jnp.sum(probs, axis=1, keepdims=True)
        mixed = (f32_dot(probs.astype(jnp.bfloat16), values) / denom).astype(jnp.bfloat16)
        for h in range(4):
            heads[rows, h * HEAD_WIDTH : (h + 1) * HEAD_WIDTH] = mixed[h * TOK : (h + 1) * TOK]
    out[...] = (f32_dot(heads[:, :256], w_own[...]) + f32_dot(heads[:, 256:], w_other[...])).astype(
        jnp.bfloat16
    )


def attend(core, q_own, q_other, kv, w_own, w_other):
    return pl.pallas_call(
        attend_kernel,
        out_shape=jax.ShapeDtypeStruct((4 * TOK, D), jnp.bfloat16),
        in_specs=[pl.BlockSpec(memory_space=pltpu.SMEM)] + whole(5),
        out_specs=whole(1)[0],
        scratch_shapes=[pltpu.VMEM((4 * TOK, 512), jnp.bfloat16)],
        compiler_params=pltpu.CompilerParams(vmem_limit_bytes=32 * MIB),
        cost_estimate=pl.CostEstimate(flops=10**9, bytes_accessed=4 * MIB, transcendentals=MIB),
        name="attend",
    )(core, q_own, q_other, kv, w_own, w_other)


def routing_kernel(routes, weights, select, combine_hi, combine_lo):
    expert = iota((TOK, EXPERTS), 1)
    routed = jnp.zeros((TOK, EXPERTS), jnp.float32)
    weight = jnp.zeros((TOK, EXPERTS), jnp.float32)
    for k in range(8):
        named = routes[:, k : k + 1] == expert
        routed = jnp.where(named, 1.0, routed)
        weight = jnp.where(named, weights[:, k : k + 1], weight)
    before = (iota((TOK, TOK), 1) < iota((TOK, TOK), 0)).astype(jnp.bfloat16)
    place = f32_dot(before, routed.astype(jnp.bfloat16))
    place = jnp.where(routed > 0, place, -1.0)
    identity = (iota((TOK, TOK), 1) == iota((TOK, TOK), 0)).astype(jnp.bfloat16)
    place_t = lax.dot_general(
        place.astype(jnp.bfloat16), identity, (((0,), (0,)), ((), ())), preferred_element_type=jnp.float32
    )

    def offset(part_slot, column):
        part = (part_slot * 205) >> 11
        slot = part_slot - part * CAP
        return jnp.where(part == (column >> 6), -slot, 100).astype(jnp.float32)

    left = iota((ROWS, 128), 0)
    left_expert = (left * 52429) >> 21
    column = iota((ROWS, 128), 1)
    spread = ((column == left_expert) | (column == left - left_expert * BLOCK + EXPERTS)).astype(jnp.bfloat16)
    table = jnp.concatenate(
        [jnp.concatenate([place_t] * PARTS, axis=1), offset(iota((64, LANES), 0), iota((64, LANES), 1))], axis=0
    ).astype(jnp.bfloat16)
    select[...] = (f32_dot(spread, table) == 0).astype(jnp.bfloat16)

    right = iota((128, ROWS), 1)
    right_expert = (right * 52429) >> 21
    row = iota((128, ROWS), 0)
    spread_t = ((row == right_expert) | (row == right - right_expert * BLOCK + EXPERTS)).astype(jnp.bfloat16)
    table_t = jnp.concatenate(
        [jnp.concatenate([place] * PARTS, axis=0), offset(iota((LANES, 64), 1), iota((LANES, 64), 0))], axis=1
    ).astype(jnp.bfloat16)
    chosen = f32_dot(table_t, spread_t) == 0
    high = weight.astype(jnp.bfloat16)
    low = (weight - high.astype(jnp.float32)).astype(jnp.bfloat16)
    for part, ref in ((high, combine_hi), (low, combine_lo)):
        part = part.astype(jnp.float32)
        wide = jnp.concatenate(
            [jnp.concatenate([part] * PARTS, axis=0), jnp.zeros((LANES, 64), jnp.float32)], axis=1
        ).astype(jnp.bfloat16)
        ref[...] = jnp.where(chosen, f32_dot(wide, spread_t), 0.0).astype(jnp.bfloat16)


def routing(routes, weights):
    return pl.pallas_call(
        routing_kernel,
        out_shape=[
            jax.ShapeDtypeStruct((ROWS, LANES), jnp.bfloat16),
            jax.ShapeDtypeStruct((LANES, ROWS), jnp.bfloat16),
            jax.ShapeDtypeStruct((LANES, ROWS), jnp.bfloat16),
        ],
        in_specs=whole(2),
        out_specs=whole(3),
        compiler_params=pltpu.CompilerParams(vmem_limit_bytes=32 * MIB),
        cost_estimate=pl.CostEstimate(flops=10**9, bytes_accessed=4 * MIB, transcendentals=0),
        name="routing",
    )(routes, weights)


def pack_kernel(shares, hidden, gain, select, rows, residual_out):
    residual = hidden[...].astype(jnp.float32)
    for index in range(4):
        residual = residual + shares[index * TOK : (index + 1) * TOK].astype(jnp.float32)
    residual_out[...] = residual
    scale = lax.rsqrt(jnp.mean(residual * residual, axis=1, keepdims=True) + NORM_EPSILON)
    normed = (residual * scale * gain[...]).astype(jnp.bfloat16)
    tall = jnp.concatenate([normed[:, part * WIDTH : (part + 1) * WIDTH] for part in range(PARTS)], axis=0)
    rows[...] = f32_dot(select[...], tall).astype(jnp.bfloat16)


def pack(shares, hidden, gain, select):
    return pl.pallas_call(
        pack_kernel,
        out_shape=[
            jax.ShapeDtypeStruct((ROWS, WIDTH), jnp.bfloat16),
            jax.ShapeDtypeStruct((TOK, D), jnp.float32),
        ],
        in_specs=whole(4),
        out_specs=whole(2),
        compiler_params=pltpu.CompilerParams(vmem_limit_bytes=32 * MIB),
        cost_estimate=pl.CostEstimate(flops=10**9, bytes_accessed=6 * MIB, transcendentals=64),
        name="pack",
    )(shares, hidden, gain, select)


def order_matrix(inverse):
    size = GROUP * BLOCK
    from_dim, to_dim = (1, 0) if not inverse else (0, 1)
    moved = iota((size, size), to_dim)
    part = (moved * 52429) >> 21
    within = moved - part * (GROUP * CAP)
    source = (within * 205) >> 11
    slot = within - source * CAP
    return (iota((size, size), from_dim) == source * BLOCK + part * CAP + slot).astype(jnp.bfloat16)


def experts_kernel(rows, gate_up, down, out, ordered, activation):
    size = GROUP * BLOCK
    part_rows = GROUP * CAP
    forth = order_matrix(False)
    for pair in range(EXPERTS // GROUP // 2):
        first = pair * 2 * size
        a = f32_dot(forth, rows[first : first + size])
        b = f32_dot(forth, rows[first + size : first + 2 * size])
        for part in range(PARTS):
            piece = slice(part * part_rows, (part + 1) * part_rows)
            ordered[
                pair * 2 * part_rows : (pair + 1) * 2 * part_rows, part * WIDTH : (part + 1) * WIDTH
            ] = jnp.concatenate([a[piece], b[piece]], axis=0).astype(jnp.bfloat16)
    both = f32_dot(ordered[...], gate_up[...])
    gate = both[:, :FF]
    activation[...] = (gate / (1.0 + jnp.exp(-gate)) * both[:, FF:]).astype(jnp.bfloat16)
    for part in range(PARTS):
        columns = slice(part * WIDTH, (part + 1) * WIDTH)
        ordered[:, columns] = lax.dot_general(
            activation[...], down[columns], (((1,), (1,)), ((), ())), preferred_element_type=jnp.float32
        ).astype(jnp.bfloat16)
    back = order_matrix(True)
    for pair in range(EXPERTS // GROUP // 2):
        first = pair * 2 * size
        pieces = [
            ordered[pair * 2 * part_rows : (pair + 1) * 2 * part_rows, part * WIDTH : (part + 1) * WIDTH].astype(
                jnp.float32
            )
            for part in range(PARTS)
        ]
        for half in range(2):
            part_slice = slice(half * part_rows, (half + 1) * part_rows)
            stacked = jnp.concatenate([piece[part_slice] for piece in pieces], axis=0).astype(jnp.bfloat16)
            out[first + half * size : first + (half + 1) * size] = f32_dot(back, stacked).astype(jnp.bfloat16)


def experts(rows, gate_up, down):
    return pl.pallas_call(
        experts_kernel,
        out_shape=jax.ShapeDtypeStruct((ROWS, WIDTH), jnp.bfloat16),
        in_specs=whole(3),
        out_specs=whole(1)[0],
        scratch_shapes=[
            pltpu.VMEM((EXPERTS * CAP, D), jnp.bfloat16),
            pltpu.VMEM((EXPERTS * CAP, FF), jnp.bfloat16),
        ],
        compiler_params=pltpu.CompilerParams(vmem_limit_bytes=40 * MIB),
        cost_estimate=pl.CostEstimate(flops=4 * 10**9, bytes_accessed=10 * MIB, transcendentals=MIB // 4),
        name="experts",
    )(rows, gate_up, down)


def combine_kernel(results, residual, combine_hi, combine_lo, out):
    total = f32_dot(combine_hi[...], results[...]) + f32_dot(combine_lo[...], results[...])
    for part in range(PARTS):
        columns = slice(part * WIDTH, (part + 1) * WIDTH)
        out[:, columns] = (residual[:, columns] + total[part * TOK : (part + 1) * TOK]).astype(jnp.bfloat16)


def combine(results, residual, combine_hi, combine_lo):
    return pl.pallas_call(
        combine_kernel,
        out_shape=jax.ShapeDtypeStruct((TOK, D), jnp.bfloat16),
        in_specs=whole(4),
        out_specs=whole(1)[0],
        compiler_params=pltpu.CompilerParams(vmem_limit_bytes=32 * MIB),
        cost_estimate=pl.CostEstimate(flops=2 * 10**9, bytes_accessed=8 * MIB, transcendentals=0),
        name="combine",
    )(results, residual, combine_hi, combine_lo)


def on_device(
    queries,
    cache_kv,
    new_key_values,
    hidden,
    out_weight,
    norm_gain,
    routes,
    gate_weights,
    gate_up,
    down_proj,
):
    core = lax.axis_index("core")
    swap = [(0, 1), (1, 0)]
    kv_rows = jnp.concatenate([cache_kv[0], new_key_values[0]], axis=0)
    by_head = [
        jnp.concatenate([kv_rows[:, g * 128 : (g + 1) * 128], kv_rows[:, (2 + g) * 128 : (3 + g) * 128]], axis=1)
        for g in range(2)
    ]
    kv = lax.all_to_all(jnp.stack([by_head[0]] * 4 + [by_head[1]] * 4), CTX, 0, 0, tiled=True).reshape(KEYS, 256)
    by_side = queries[0].reshape(4, 2, TOK, 256)
    q_own = lax.dynamic_index_in_dim(by_side, core, 1, False).reshape(4 * TOK, 256)
    q_away = lax.dynamic_index_in_dim(by_side, 1 - core, 1, False).reshape(4 * TOK, 256)
    q_other = lax.ppermute(q_away, "core", swap)
    w_other = lax.ppermute(out_weight, "core", swap)
    select, combine_hi, combine_lo = routing(routes[0], gate_weights[0])
    full_gate_up = lax.all_gather(gate_up[0], CTX, axis=0, tiled=True)
    full_down = lax.all_gather(down_proj[0], CTX, axis=0, tiled=True)

    partial = attend(core.reshape(1), q_own, q_other, kv, out_weight, w_other)
    shares = lax.all_to_all(partial.reshape(4, TOK, D), "yh", 0, 0, tiled=True).reshape(4 * TOK, D)
    rows, residual = pack(shares, hidden[0], norm_gain.reshape(1, D), select)
    arrived = lax.all_to_all(rows.reshape(EXPERTS, BLOCK, WIDTH), EXP, 0, 0, tiled=True)
    outputs = experts(arrived.reshape(ROWS, WIDTH), full_gate_up, full_down)
    results = lax.all_to_all(outputs.reshape(EXPERTS, BLOCK, WIDTH), EXP, 0, 0, tiled=True)
    return combine(results.reshape(ROWS, WIDTH), residual, combine_hi, combine_lo)[None]


def solution(mesh):
    parts = Mesh(mesh.devices.reshape(4, 2, 4, 8, 2), ("yh", "core", "x", "z", "yl"))
    rows = P(EXP, CTX, None)
    return jax.shard_map(
        on_device,
        mesh=parts,
        in_specs=(
            P(EXP, None, CTX),
            rows,
            rows,
            rows,
            P(CTX, None),
            P(),
            rows,
            rows,
            rows,
            rows,
        ),
        out_specs=rows,
        check_vma=False,
    )
```

time: 371 us -> 245 us (0.66)
  the two profiles are of different devices: /device:TPU:25 before, /device:TPU:24 now
where the time goes in v1:
time: 245 us; the launch traced here: 244 us
  waiting for transfers between devices  94.5 us (39%)
  blocking collectives  69.7 us (28%)
  starting transfers between devices  36.8 us (15%)
  Pallas kernels  15.8 us (6%)
  between operations  13.5 us (6%)
  local copies, waits for them, and re-layouts  9.11 us (4%)
  other arithmetic  4.72 us (2%)
    all_to_all x1, blocking collectives, on_device(): lax.all_to_all(outputs.reshape(EXPERTS, BLOCK, WIDTH), EXP, 0, 0, tiled=T...  69.7 us
    all_to_all x1, waiting for transfers between devices, on_device(): lax.all_to_all(rows.reshape(EXPERTS, BLOCK, WIDTH), EXP, 0, 0, tiled=True)  39.9 us
    all_gather x1, waiting for transfers between devices, on_device(): full_gate_up = lax.all_gather(gate_up[0], CTX, axis=0, tiled=True)  24.2 us
    all_to_all x1, starting transfers between devices, on_device(): lax.all_to_all(rows.reshape(EXPERTS, BLOCK, WIDTH), EXP, 0, 0, tiled=True)  19 us
    all_to_all x1, waiting for transfers between devices, on_device(): lax.all_to_all(partial.reshape(4, TOK, D), 'yh', 0, 0, tiled=True)  16 us
    all_to_all x1, waiting for transfers between devices, on_device(): lax.all_to_all(jnp.stack([by_head[0]] * 4 + [by_head[1]] * 4), CTX, 0, 0,...  12.5 us
    unnamed x30, local copies, waits for them, and re-layouts  8.46 us
    all_to_all x1, starting transfers between devices, on_device(): lax.all_to_all(partial.reshape(4, TOK, D), 'yh', 0, 0, tiled=True)  7.11 us
  transfers between devices with their start and end apart: 7, of which 5 were waited for; matrix products, arithmetic and copies ran while one was open for 3% of the time, Pallas kernels for 3%

profile of v1, /device:TPU:24, one launch (start us, length us, event | category | flops | bytes accessed | tf_op | source)
XLA Modules:
  0.0 244.2 jit_solution(14260381332685831296)
XLA Ops:
  6.5 0.0 copy-start.1
  6.5 0.0 copy-start.10
  6.5 0.0 all-gather.7.cloned.1.call-start
  6.5 2.0 collective-permute-start.1
  8.6 0.0 all-gather.7.cloned.1.call-update
  8.6 0.8 fusion.5
  9.4 0.6 constant_dynamic-update-slice_fusion.7
  10.1 0.6 constant_dynamic-update-slice_fusion.6
  10.7 0.6 constant_dynamic-update-slice_fusion.5
  11.3 0.6 constant_dynamic-update-slice_fusion.4
  11.9 1.4 constant_dynamic-update-slice_fusion.3
  13.3 0.6 constant_dynamic-update-slice_fusion.2
  14.0 0.6 constant_dynamic-update-slice_fusion.1
  14.6 0.6 constant_dynamic-update-slice_fusion
  15.2 6.6 %all-to-all-start = ((bf16[8,128,256]{2,1,0:T(8,128)(2,1)}), bf16[8,128,256]{2,1,0:T(8,128)(2,1)S(1)}, u32[]{:S(2)}, u32[]{:S(2)}) async-start(bf16[8,128,256]{2,1,0:T(8,128)(2,1)} %constant_dynamic-update-slice_fusion), calls=%async_computation | async-start | bytes 1048576 | tf_op jit(solution)/shard_map/all_to_all | solution.py:273
  21.9 0.0 copy-done.10
  21.9 2.1 collective-permute-start
  24.0 1.2 collective-permute-done.q_other
  25.1 12.5 %all-to-all-done = bf16[8,128,256]{2,1,0:T(8,128)(2,1)S(1)} async-done(((bf16[8,128,256]{2,1,0:T(8,128)(2,1)}), bf16[8,128,256]{2,1,0:T(8,128)(2,1)S(1)}, u32[]{:S(2)}, u32[]{:S(2)}) %all-to-all-start) | async-done | bytes 524320 | tf_op jit(solution)/shard_map/all_to_all | solution.py:273
  37.6 0.0 collective-permute-done.1.w_other
  37.6 0.0 copy-done.1
  37.7 0.0 copy-start.11
  37.7 0.0 copy-start.12
  37.7 3.8 %attend.1 = bf16[256,2048]{1,0:T(8,128)(2,1)} custom-call(s32[1]{0:T(128)} %bitcast.core_ref, bf16[256,256]{1,0:T(8,128)(2,1)S(1)} %bitcast.43, bf16[256,256]{1,0:T(8,128)(2,1)S(1)} %collective-permute-done.q_other, bf16[1024,256]{1,0:T(8,128)(2,1)S(1)} %bitcast.41, bf16[256,2048]{1,0:T(8,128)(2,1)S(1)} %copy-done.1, ...), custom_call_target="tpu_custom_call" | custom-call | flops 1000000000 | bytes 4194304 | tf_op jit(solution)/shard_map/attend/pallas_call | solution.py:70
  41.4 0.0 copy-start.4
  41.4 0.0 copy-start.5
  41.4 7.1 %all-to-all-start.1 = ((bf16[4,64,2048]{2,1,0:T(8,128)(2,1)}), bf16[4,64,2048]{2,1,0:T(8,128)(2,1)S(1)}, u32[]{:S(2)}, u32[]{:S(2)}) async-start(bf16[4,64,2048]{2,1,0:T(8,128)(2,1)} %bitcast.9), calls=%async_computation.1 | async-start | bytes 2097152 | tf_op jit(solution)/shard_map/all_to_all | solution.py:284
  48.6 0.0 all-gather.5.cloned.1.call-start
  48.6 0.7 all-gather.5.cloned.1.call-update
  49.3 0.0 copy-done.11
  49.3 0.1 copy.13
  49.4 0.0 copy-done.12
  49.4 0.1 copy.14
  49.5 2.5 %routing.1 = (bf16[2560,256]{1,0:T(8,128)(2,1)S(1)}, bf16[256,2560]{1,0:T(8,128)(2,1)S(1)}, bf16[256,2560]{1,0:T(8,128)(2,1)S(1)}) custom-call(s32[64,8]{1,0:T(8,128)S(1)} %bitcast.44, f32[64,8]{1,0:T(8,128)S(1)} %bitcast.45), custom_call_target="tpu_custom_call" | custom-call | flops 1000000000 | bytes 4194304 | tf_op jit(solution)/shard_map/routing/pallas_call | solution.py:131
  52.0 0.0 copy-start.6
  52.0 1.2 copy-done.6
  53.1 0.0 copy-start.8
  53.1 1.1 copy-done.8
  54.2 16.0 %all-to-all-done.1 = bf16[4,64,2048]{2,1,0:T(8,128)(2,1)S(1)} async-done(((bf16[4,64,2048]{2,1,0:T(8,128)(2,1)}), bf16[4,64,2048]{2,1,0:T(8,128)(2,1)S(1)}, u32[]{:S(2)}, u32[]{:S(2)}) %all-to-all-start.1) | async-done | bytes 1048608 | tf_op jit(solution)/shard_map/all_to_all | solution.py:284
  70.2 0.0 copy-done.4
  70.2 0.0 copy-done.5
  70.2 1.1 pack.1
  71.3 0.0 copy-start
  71.3 1.5 copy-done
  72.8 19.0 %all-to-all-start.2 = ((bf16[64,40,512]{2,1,0:T(8,128)(2,1)}), bf16[64,40,512]{2,1,0:T(8,128)(2,1)S(1)}, u32[]{:S(2)}, u32[]{:S(2)}) async-start(bf16[64,40,512]{2,1,0:T(8,128)(2,1)} %bitcast.38), calls=%async_computation.2 | async-start | bytes 5242880 | tf_op jit(solution)/shard_map/all_to_all | solution.py:286
  91.8 0.0 all-gather.7.cloned.1.call-done
  91.9 24.2 %all-gather.5.cloned.1.call-done = bf16[1,2048,768]{2,1,0:T(8,128)(2,1)} async-done(((bf16[1,256,768]{2,1,0:T(8,128)(2,1)}), bf16[1,2048,768]{2,1,0:T(8,128)(2,1)}) %all-gather.5.cloned.1.call-update) | async-done | bytes 3145744 | tf_op jit(solution)/shard_map/all_gather | solution.py:280
  116.0 39.9 %all-to-all-done.2 = bf16[64,40,512]{2,1,0:T(8,128)(2,1)S(1)} async-done(((bf16[64,40,512]{2,1,0:T(8,128)(2,1)}), bf16[64,40,512]{2,1,0:T(8,128)(2,1)S(1)}, u32[]{:S(2)}, u32[]{:S(2)}) %all-to-all-start.2) | async-done | bytes 2621472 | tf_op jit(solution)/shard_map/all_to_all | solution.py:286
  155.9 0.0 copy-start.2
  155.9 1.9 copy-done.2
  157.8 0.0 copy-start.3
  157.8 1.4 copy-done.3
  159.2 6.2 %experts.1 = bf16[2560,512]{1,0:T(8,128)(2,1)S(1)} custom-call(bf16[2560,512]{1,0:T(8,128)(2,1)S(1)} %bitcast.37, bf16[2048,768]{1,0:T(8,128)(2,1)S(1)} %bitcast.46, bf16[2048,384]{1,0:T(8,128)(2,1)S(1)} %bitcast.47), custom_call_target="tpu_custom_call" | custom-call | flops 4000000000 | bytes 10485760 | tf_op jit(solution)/shard_map/experts/pallas_call | solution.py:220
  165.4 0.0 copy-start.7
  165.4 0.0 copy-start.9
  165.4 69.7 %all_to_all.20 = bf16[64,40,512]{2,1,0:T(8,128)(2,1)S(1)} all-to-all(bf16[64,40,512]{2,1,0:T(8,128)(2,1)S(1)} %bitcast.40), channel_id=1, replica_groups=mesh['yh'=4,'core'=2,'x'=4,'z'=8,'yl'=2] {'x','z','yl'}, dimensions={0} | all-to-all | bytes 5242880 | tf_op jit(solution)/shard_map/all_to_all | solution.py:288
  235.2 0.0 copy-done.7
  235.2 0.0 copy-done.9
  235.2 2.2 combine.1
  (1 shorter events, 0.0 us)
Async XLA Ops:
  6.5 31.1 %copy-start.1 = (bf16[256,2048]{1,0:T(8,128)(2,1)S(1)}, bf16[256,2048]{1,0:T(8,128)(2,1)}, u32[]{:S(2)}) copy-start(bf16[256,2048]{1,0:T(8,128)(2,1)} %w_own.1) | copy-start | bytes 3145732
  6.5 15.3 %copy-start.10 = (bf16[1,512,256]{2,1,0:T(8,128)(2,1)S(1)}, bf16[1,512,256]{2,1,0:T(8,128)(2,1)}, u32[]{:S(2)}) copy-start(bf16[1,512,256]{2,1,0:T(8,128)(2,1)} %param.10) | copy-start | bytes 786436
  6.5 85.3 %all-gather.7.cloned.1.call-start = ((), (), s32[]{:S(2)}) async-start(), calls=%async_computation.5 | async-start | bytes 1769472 | tf_op jit(solution)/shard_map/all_gather | solution.py:281
  6.5 31.1 %collective-permute-start.1 = (bf16[256,2048]{1,0:T(8,128)(2,1)}, bf16[256,2048]{1,0:T(8,128)(2,1)S(1)}, u32[]{:S(2)}, u32[]{:S(2)}) collective-permute-start(bf16[256,2048]{1,0:T(8,128)(2,1)} %w_own.1), channel_id=1, source_target_pairs={{0,64},{64,0},{1,65},{65,1},{2,66},{66,2},{3,67},{67,3},{4,68},{68... | collective-permute-start | bytes 3145736 | tf_op jit(solution)/shard_map/ppermute | solution.py:278
  15.2 22.4 %all-to-all-start = ((bf16[8,128,256]{2,1,0:T(8,128)(2,1)}), bf16[8,128,256]{2,1,0:T(8,128)(2,1)S(1)}, u32[]{:S(2)}, u32[]{:S(2)}) async-start(bf16[8,128,256]{2,1,0:T(8,128)(2,1)} %constant_dynamic-update-slice_fusion), calls=%async_computation | async-start | bytes 1048576 | tf_op jit(solution)/shard_map/all_to_all | solution.py:273
  21.9 3.2 %collective-permute-start = (bf16[256,256]{1,0:T(8,128)(2,1)S(1)}, bf16[256,256]{1,0:T(8,128)(2,1)S(1)}, u32[]{:S(2)}, u32[]{:S(2)}) collective-permute-start(bf16[256,256]{1,0:T(8,128)(2,1)S(1)} %bitcast.55), channel_id=1, source_target_pairs={{0,64},{64,0},{1,65},{65,1},{2,66},{66,2},{3,67},{67,3},{4,68},{68... | collective-permute-start | bytes 393224 | tf_op jit(solution)/shard_map/ppermute | solution.py:277
  37.7 11.6 %copy-start.11 = (s32[1,64,8]{1,2,0:T(8,128)S(1)}, s32[1,64,8]{1,2,0:T(8,128)}, u32[]{:S(2)}) copy-start(s32[1,64,8]{1,2,0:T(8,128)} %param.16) | copy-start | bytes 6148
  37.7 11.7 %copy-start.12 = (f32[1,64,8]{1,2,0:T(8,128)S(1)}, f32[1,64,8]{1,2,0:T(8,128)}, u32[]{:S(2)}) copy-start(f32[1,64,8]{1,2,0:T(8,128)} %param.17) | copy-start | bytes 6148
  41.4 28.8 %copy-start.4 = (bf16[1,64,2048]{2,1,0:T(8,128)(2,1)S(1)}, bf16[1,64,2048]{2,1,0:T(8,128)(2,1)}, u32[]{:S(2)}) copy-start(bf16[1,64,2048]{2,1,0:T(8,128)(2,1)} %param.13) | copy-start | bytes 786436
  41.4 28.8 %copy-start.5 = (f32[2048]{0:T(1024)S(1)}, f32[2048]{0:T(1024)}, u32[]{:S(2)}) copy-start(f32[2048]{0:T(1024)} %param.15) | copy-start | bytes 24580
  41.4 28.8 %all-to-all-start.1 = ((bf16[4,64,2048]{2,1,0:T(8,128)(2,1)}), bf16[4,64,2048]{2,1,0:T(8,128)(2,1)S(1)}, u32[]{:S(2)}, u32[]{:S(2)}) async-start(bf16[4,64,2048]{2,1,0:T(8,128)(2,1)} %bitcast.9), calls=%async_computation.1 | async-start | bytes 2097152 | tf_op jit(solution)/shard_map/all_to_all | solution.py:284
  48.6 67.5 %all-gather.5.cloned.1.call-start = ((), (), s32[]{:S(2)}) async-start(), calls=%async_computation.4 | async-start | bytes 3538944 | tf_op jit(solution)/shard_map/all_gather | solution.py:280
  52.0 1.2 copy-start.6
  53.1 1.1 copy-start.8
  71.3 1.5 copy-start
  72.8 83.0 %all-to-all-start.2 = ((bf16[64,40,512]{2,1,0:T(8,128)(2,1)}), bf16[64,40,512]{2,1,0:T(8,128)(2,1)S(1)}, u32[]{:S(2)}, u32[]{:S(2)}) async-start(bf16[64,40,512]{2,1,0:T(8,128)(2,1)} %bitcast.38), calls=%async_computation.2 | async-start | bytes 5242880 | tf_op jit(solution)/shard_map/all_to_all | solution.py:286
  155.9 1.9 copy-start.2
  157.8 1.4 copy-start.3
  165.4 69.8 %copy-start.7 = (bf16[256,2560]{1,0:T(8,128)(2,1)S(1)}, bf16[256,2560]{1,0:T(8,128)(2,1)}, u32[]{:S(2)}) copy-start(bf16[256,2560]{1,0:T(8,128)(2,1)} %copy-done.6) | copy-start | bytes 3932164
  165.4 69.8 %copy-start.9 = (bf16[256,2560]{1,0:T(8,128)(2,1)S(1)}, bf16[256,2560]{1,0:T(8,128)(2,1)}, u32[]{:S(2)}) copy-start(bf16[256,2560]{1,0:T(8,128)(2,1)} %copy-done.8) | copy-start | bytes 3932164
Sparse Core Ops, SparseCore 0:
  9.5 45.9 all-gather.6
  57.6 58.3 all-gather.4

commit v2 on v1

--- a/solution.py
+++ b/solution.py
@@ -38,11 +38,60 @@
     return lax.broadcasted_iota(jnp.int32, shape, dim)
 
 
+def prepare_kernel(core_ref, cache, new, queries, kv_out, q_own, q_away, held_kv, held_q, arrivals):
+    fetches = [
+        pltpu.make_async_copy(cache, held_kv.at[0], arrivals.at[0]),
+        pltpu.make_async_copy(new, held_kv.at[1], arrivals.at[1]),
+        pltpu.make_async_copy(queries, held_q, arrivals.at[2]),
+    ]
+    for fetch in fetches:
+        fetch.start()
+    for fetch in fetches[:2]:
+        fetch.wait()
+    for head in range(2):
+        for index in range(2):
+            for half in range(2):
+                rows = slice(half * TOK, (half + 1) * TOK)
+                kv_out[head * 2 + index, rows, :HEAD_WIDTH] = held_kv[
+                    half, :, head * HEAD_WIDTH : (head + 1) * HEAD_WIDTH
+                ]
+                kv_out[head * 2 + index, rows, HEAD_WIDTH:] = held_kv[
+                    half, :, (2 + head) * HEAD_WIDTH : (3 + head) * HEAD_WIDTH
+                ]
+    fetches[2].wait()
+    first = core_ref[0] == 0
+    for block in range(4):
+        rows = slice(block * TOK, (block + 1) * TOK)
+        low = held_q[block * 2 * TOK : (block * 2 + 1) * TOK]
+        high = held_q[(block * 2 + 1) * TOK : (block + 1) * 2 * TOK]
+        q_own[rows] = jnp.where(first, low, high)
+        q_away[rows] = jnp.where(first, high, low)
+
+
+def prepare(core, cache, new, queries):
+    side = jax.ShapeDtypeStruct((4 * TOK, 256), jnp.bfloat16)
+    return pl.pallas_call(
+        prepare_kernel,
+        out_shape=[jax.ShapeDtypeStruct((4, 2 * TOK, 256), jnp.bfloat16), side, side],
+        in_specs=[pl.BlockSpec(memory_space=pltpu.SMEM)] + [pl.BlockSpec(memory_space=pl.ANY)] * 3,
+        out_specs=whole(3),
+        scratch_shapes=[
+            pltpu.VMEM((2, TOK, 512), jnp.bfloat16),
+            pltpu.VMEM((8 * TOK, 256), jnp.bfloat16),
+            pltpu.SemaphoreType.DMA((3,)),
+        ],
+        compiler_params=pltpu.CompilerParams(vmem_limit_bytes=60 * MIB),
+        cost_estimate=pl.CostEstimate(flops=0, bytes_accessed=MIB, transcendentals=0),
+        name="prepare",
+    )(core, cache, new, queries)
+
+
 def attend_kernel(core_ref, q_own, q_other, kv, w_own, w_other, out, heads):
     base = core_ref[0] * TOK
     key_index = iota((4 * TOK, KEYS), 1)
     within = key_index & 127
-    key_pos = jnp.where(within < TOK, -1, ((key_index >> 7) * TOK) + within - TOK)
+    owner = ((key_index >> 7) & 3) * 2 + (key_index >> 9)
+    key_pos = jnp.where(within < TOK, -1, owner * TOK + within - TOK)
     row_pos = (iota((4 * TOK, KEYS), 0) & (TOK - 1)) + base
     keys = kv[:, :HEAD_WIDTH]
     values = kv[:, HEAD_WIDTH:]
@@ -265,21 +314,14 @@
 ):
     core = lax.axis_index("core")
     swap = [(0, 1), (1, 0)]
-    kv_rows = jnp.concatenate([cache_kv[0], new_key_values[0]], axis=0)
-    by_head = [
-        jnp.concatenate([kv_rows[:, g * 128 : (g + 1) * 128], kv_rows[:, (2 + g) * 128 : (3 + g) * 128]], axis=1)
-        for g in range(2)
-    ]
-    kv = lax.all_to_all(jnp.stack([by_head[0]] * 4 + [by_head[1]] * 4), CTX, 0, 0, tiled=True).reshape(KEYS, 256)
-    by_side = queries[0].reshape(4, 2, TOK, 256)
-    q_own = lax.dynamic_index_in_dim(by_side, core, 1, False).reshape(4 * TOK, 256)
-    q_away = lax.dynamic_index_in_dim(by_side, 1 - core, 1, False).reshape(4 * TOK, 256)
+    kv_send, q_own, q_away = prepare(core.reshape(1), cache_kv[0], new_key_values[0], queries[0])
+    kv = lax.all_to_all(kv_send, "yh", 0, 0, tiled=True).reshape(KEYS // 2, 256)
+    kv = lax.all_gather(kv, "core", axis=0, tiled=True)
     q_other = lax.ppermute(q_away, "core", swap)
     w_other = lax.ppermute(out_weight, "core", swap)
     select, combine_hi, combine_lo = routing(routes[0], gate_weights[0])
     full_gate_up = lax.all_gather(gate_up[0], CTX, axis=0, tiled=True)
     full_down = lax.all_gather(down_proj[0], CTX, axis=0, tiled=True)
-
     partial = attend(core.reshape(1), q_own, q_other, kv, out_weight, w_other)
     shares = lax.all_to_all(partial.reshape(4, TOK, D), "yh", 0, 0, tiled=True).reshape(4 * TOK, D)
     rows, residual = pack(shares, hidden[0], norm_gain.reshape(1, D), select)

time: 245 us -> 238 us (0.971)
  the two profiles are of different devices: /device:TPU:24 before, /device:TPU:8 now
where the time goes in v2:
time: 238 us; the launch traced here: 237 us
  waiting for transfers between devices  96.3 us (40%)
  blocking collectives  71.5 us (30%)
  starting transfers between devices  29.2 us (12%)
  Pallas kernels  17.7 us (7%)
  between operations  13.5 us (6%)
  local copies, waits for them, and re-layouts  9.32 us (4%)
    all_to_all x1, blocking collectives, on_device(): lax.all_to_all(outputs.reshape(EXPERTS, BLOCK, WIDTH), EXP, 0, 0, tiled=T...  69.2 us
    all_to_all x1, waiting for transfers between devices, on_device(): lax.all_to_all(rows.reshape(EXPERTS, BLOCK, WIDTH), EXP, 0, 0, tiled=True)  43.6 us
    all_to_all x1, waiting for transfers between devices, on_device(): lax.all_to_all(partial.reshape(4, TOK, D), 'yh', 0, 0, tiled=True)  23 us
    all_gather x1, waiting for transfers between devices, on_device(): full_gate_up = lax.all_gather(gate_up[0], CTX, axis=0, tiled=True)  19.2 us
    all_to_all x1, starting transfers between devices, on_device(): lax.all_to_all(rows.reshape(EXPERTS, BLOCK, WIDTH), EXP, 0, 0, tiled=True)  15.3 us
    unnamed x28, local copies, waits for them, and re-layouts  9.32 us
    all_to_all x1, waiting for transfers between devices, on_device(): kv = lax.all_to_all(kv_send, 'yh', 0, 0, tiled=True).reshape(KEYS // 2, 256)  9.01 us
    pallas_call x1, Pallas kernels, experts(): pl.pallas_call(experts_kernel, out_shape=jax.ShapeDtypeStruct((ROWS, WIDT...  6.22 us
  transfers between devices with their start and end apart: 7, of which 4 were waited for; matrix products, arithmetic and copies ran while one was open for 0% of the time, Pallas kernels for 4%

profile of v2, /device:TPU:8, one launch (start us, length us, event | category | flops | bytes accessed | tf_op | source)
XLA Modules:
  0.0 237.5 jit_solution(274545836091554967)
XLA Ops:
  6.5 0.0 all-gather.7.cloned.1.call-start
  6.5 0.7 all-gather.7.cloned.1.call-update
  7.3 1.9 collective-permute-start.1
  9.2 1.8 prepare.1
  11.0 6.2 %all-to-all-start = ((bf16[4,128,256]{2,1,0:T(8,128)(2,1)}), bf16[4,128,256]{2,1,0:T(8,128)(2,1)S(1)}, u32[]{:S(2)}, u32[]{:S(2)}) async-start(bf16[4,128,256]{2,1,0:T(8,128)(2,1)} %get-tuple-element.15), calls=%async_computation | async-start | bytes 524288 | tf_op jit(solution)/shard_map/all_to_all | solution.py:318
  17.2 2.1 collective-permute-start
  19.4 9.0 %all-to-all-done = bf16[4,128,256]{2,1,0:T(8,128)(2,1)S(1)} async-done(((bf16[4,128,256]{2,1,0:T(8,128)(2,1)}), bf16[4,128,256]{2,1,0:T(8,128)(2,1)S(1)}, u32[]{:S(2)}, u32[]{:S(2)}) %all-to-all-start) | async-done | bytes 262176 | tf_op jit(solution)/shard_map/all_to_all | solution.py:318
  28.4 2.2 all_gather.9.kv
  30.6 0.0 collective-permute-done.q_other
  30.6 0.0 collective-permute-done.1.w_other
  30.6 0.0 copy-start.1
  30.6 1.2 copy-done.1
  31.8 0.0 copy-start.2
  31.8 0.9 copy-done.2
  32.7 0.0 copy-start.11
  32.7 0.0 copy-start.12
  32.7 3.8 %attend.1 = bf16[256,2048]{1,0:T(8,128)(2,1)} custom-call(s32[1]{0:T(128)} %bitcast.core_ref, bf16[256,256]{1,0:T(8,128)(2,1)S(1)} %copy-done.2, bf16[256,256]{1,0:T(8,128)(2,1)S(1)} %collective-permute-done.q_other, bf16[1024,256]{1,0:T(8,128)(2,1)S(1)} %all_gather.9.kv, bf16[256,2048]{1,0:T(8,128)(2,1)S(1)} %copy-done.1, ...), custom_call_target="tpu_custom_call" | custom-call | flops 1000000000 | bytes 4194304 | tf_op jit(solution)/shard_map/attend/pallas_call | solution.py:119
  36.5 0.0 copy-start.5
  36.5 0.0 copy-start.6
  36.5 3.6 %all-to-all-start.1 = ((bf16[4,64,2048]{2,1,0:T(8,128)(2,1)}), bf16[4,64,2048]{2,1,0:T(8,128)(2,1)S(1)}, u32[]{:S(2)}, u32[]{:S(2)}) async-start(bf16[4,64,2048]{2,1,0:T(8,128)(2,1)} %bitcast.5), calls=%async_computation.1 | async-start | bytes 2097152 | tf_op jit(solution)/shard_map/all_to_all | solution.py:326
  40.2 0.0 all-gather.5.cloned.1.call-start
  40.2 0.7 all-gather.5.cloned.1.call-update
  40.9 0.0 copy-done.11
  40.9 0.1 copy.12
  41.0 0.0 copy-done.12
  41.0 0.1 copy.11
  41.1 2.5 %routing.1 = (bf16[2560,256]{1,0:T(8,128)(2,1)S(1)}, bf16[256,2560]{1,0:T(8,128)(2,1)S(1)}, bf16[256,2560]{1,0:T(8,128)(2,1)S(1)}) custom-call(s32[64,8]{1,0:T(8,128)S(1)} %bitcast.24, f32[64,8]{1,0:T(8,128)S(1)} %bitcast.23), custom_call_target="tpu_custom_call" | custom-call | flops 1000000000 | bytes 4194304 | tf_op jit(solution)/shard_map/routing/pallas_call | solution.py:180
  43.6 0.0 copy-start.7
  43.6 1.1 copy-done.7
  44.8 0.0 copy-start.9
  44.8 1.1 copy-done.9
  45.8 23.0 %all-to-all-done.1 = bf16[4,64,2048]{2,1,0:T(8,128)(2,1)S(1)} async-done(((bf16[4,64,2048]{2,1,0:T(8,128)(2,1)}), bf16[4,64,2048]{2,1,0:T(8,128)(2,1)S(1)}, u32[]{:S(2)}, u32[]{:S(2)}) %all-to-all-start.1) | async-done | bytes 1048608 | tf_op jit(solution)/shard_map/all_to_all | solution.py:326
  68.8 0.0 copy-done.5
  68.8 0.0 copy-done.6
  68.8 1.1 pack.1
  70.0 0.0 copy-start
  70.0 1.5 copy-done
  71.5 15.3 %all-to-all-start.2 = ((bf16[64,40,512]{2,1,0:T(8,128)(2,1)}), bf16[64,40,512]{2,1,0:T(8,128)(2,1)S(1)}, u32[]{:S(2)}, u32[]{:S(2)}) async-start(bf16[64,40,512]{2,1,0:T(8,128)(2,1)} %bitcast.19), calls=%async_computation.2 | async-start | bytes 5242880 | tf_op jit(solution)/shard_map/all_to_all | solution.py:328
  86.8 0.0 all-gather.7.cloned.1.call-done
  86.8 19.2 %all-gather.5.cloned.1.call-done = bf16[1,2048,768]{2,1,0:T(8,128)(2,1)} async-done(((bf16[1,256,768]{2,1,0:T(8,128)(2,1)}), bf16[1,2048,768]{2,1,0:T(8,128)(2,1)}) %all-gather.5.cloned.1.call-update) | async-done | bytes 3145744 | tf_op jit(solution)/shard_map/all_gather | solution.py:323
  106.0 43.6 %all-to-all-done.2 = bf16[64,40,512]{2,1,0:T(8,128)(2,1)S(1)} async-done(((bf16[64,40,512]{2,1,0:T(8,128)(2,1)}), bf16[64,40,512]{2,1,0:T(8,128)(2,1)S(1)}, u32[]{:S(2)}, u32[]{:S(2)}) %all-to-all-start.2) | async-done | bytes 2621472 | tf_op jit(solution)/shard_map/all_to_all | solution.py:328
  149.6 0.0 copy-start.3
  149.6 1.9 copy-done.3
  151.5 0.0 copy-start.4
  151.5 1.4 copy-done.4
  152.9 6.2 %experts.1 = bf16[2560,512]{1,0:T(8,128)(2,1)S(1)} custom-call(bf16[2560,512]{1,0:T(8,128)(2,1)S(1)} %bitcast.18, bf16[2048,768]{1,0:T(8,128)(2,1)S(1)} %bitcast.25, bf16[2048,384]{1,0:T(8,128)(2,1)S(1)} %bitcast.26), custom_call_target="tpu_custom_call" | custom-call | flops 4000000000 | bytes 10485760 | tf_op jit(solution)/shard_map/experts/pallas_call | solution.py:269
  159.2 0.0 copy-start.8
  159.2 0.0 copy-start.10
  159.2 69.2 %all_to_all.20 = bf16[64,40,512]{2,1,0:T(8,128)(2,1)S(1)} all-to-all(bf16[64,40,512]{2,1,0:T(8,128)(2,1)S(1)} %bitcast.21), channel_id=1, replica_groups=mesh['yh'=4,'core'=2,'x'=4,'z'=8,'yl'=2] {'x','z','yl'}, dimensions={0} | all-to-all | bytes 5242880 | tf_op jit(solution)/shard_map/all_to_all | solution.py:330
  228.4 0.0 copy-done.8
  228.4 0.0 copy-done.10
  228.4 2.2 combine.1
Async XLA Ops:
  6.5 80.3 %all-gather.7.cloned.1.call-start = ((), (), s32[]{:S(2)}) async-start(), calls=%async_computation.5 | async-start | bytes 1769472 | tf_op jit(solution)/shard_map/all_gather | solution.py:324
  7.3 23.3 %collective-permute-start.1 = (bf16[256,2048]{1,0:T(8,128)(2,1)}, bf16[256,2048]{1,0:T(8,128)(2,1)S(1)}, u32[]{:S(2)}, u32[]{:S(2)}) collective-permute-start(bf16[256,2048]{1,0:T(8,128)(2,1)} %w_own.1), channel_id=1, source_target_pairs={{0,64},{64,0},{1,65},{65,1},{2,66},{66,2},{3,67},{67,3},{4,68},{68... | collective-permute-start | bytes 3145736 | tf_op jit(solution)/shard_map/ppermute | solution.py:321
  11.0 17.3 %all-to-all-start = ((bf16[4,128,256]{2,1,0:T(8,128)(2,1)}), bf16[4,128,256]{2,1,0:T(8,128)(2,1)S(1)}, u32[]{:S(2)}, u32[]{:S(2)}) async-start(bf16[4,128,256]{2,1,0:T(8,128)(2,1)} %get-tuple-element.15), calls=%async_computation | async-start | bytes 524288 | tf_op jit(solution)/shard_map/all_to_all | solution.py:318
  17.2 13.4 %collective-permute-start = (bf16[256,256]{1,0:T(8,128)(2,1)}, bf16[256,256]{1,0:T(8,128)(2,1)S(1)}, u32[]{:S(2)}, u32[]{:S(2)}) collective-permute-start(bf16[256,256]{1,0:T(8,128)(2,1)} %get-tuple-element.14), channel_id=1, source_target_pairs={{0,64},{64,0},{1,65},{65,1},{2,66},{66,2},{3,67},{67,3},{4,68},{68... | collective-permute-start | bytes 393224 | tf_op jit(solution)/shard_map/ppermute | solution.py:320
  30.6 1.2 copy-start.1
  31.8 0.9 copy-start.2
  32.7 8.2 %copy-start.11 = (f32[1,64,8]{1,2,0:T(8,128)S(1)}, f32[1,64,8]{1,2,0:T(8,128)}, u32[]{:S(2)}) copy-start(f32[1,64,8]{1,2,0:T(8,128)} %param.17) | copy-start | bytes 6148
  32.7 8.3 %copy-start.12 = (s32[1,64,8]{1,2,0:T(8,128)S(1)}, s32[1,64,8]{1,2,0:T(8,128)}, u32[]{:S(2)}) copy-start(s32[1,64,8]{1,2,0:T(8,128)} %param.16) | copy-start | bytes 6148
  36.5 32.3 %copy-start.5 = (bf16[1,64,2048]{2,1,0:T(8,128)(2,1)S(1)}, bf16[1,64,2048]{2,1,0:T(8,128)(2,1)}, u32[]{:S(2)}) copy-start(bf16[1,64,2048]{2,1,0:T(8,128)(2,1)} %param.13) | copy-start | bytes 786436
  36.5 32.3 %copy-start.6 = (f32[2048]{0:T(1024)S(1)}, f32[2048]{0:T(1024)}, u32[]{:S(2)}) copy-start(f32[2048]{0:T(1024)} %param.15) | copy-start | bytes 24580
  36.5 32.3 %all-to-all-start.1 = ((bf16[4,64,2048]{2,1,0:T(8,128)(2,1)}), bf16[4,64,2048]{2,1,0:T(8,128)(2,1)S(1)}, u32[]{:S(2)}, u32[]{:S(2)}) async-start(bf16[4,64,2048]{2,1,0:T(8,128)(2,1)} %bitcast.5), calls=%async_computation.1 | async-start | bytes 2097152 | tf_op jit(solution)/shard_map/all_to_all | solution.py:326
  40.2 65.8 %all-gather.5.cloned.1.call-start = ((), (), s32[]{:S(2)}) async-start(), calls=%async_computation.4 | async-start | bytes 3538944 | tf_op jit(solution)/shard_map/all_gather | solution.py:323
  43.6 1.2 copy-start.7
  44.8 1.1 copy-start.9
  70.0 1.5 copy-start
  71.5 78.2 %all-to-all-start.2 = ((bf16[64,40,512]{2,1,0:T(8,128)(2,1)}), bf16[64,40,512]{2,1,0:T(8,128)(2,1)S(1)}, u32[]{:S(2)}, u32[]{:S(2)}) async-start(bf16[64,40,512]{2,1,0:T(8,128)(2,1)} %bitcast.19), calls=%async_computation.2 | async-start | bytes 5242880 | tf_op jit(solution)/shard_map/all_to_all | solution.py:328
  149.6 1.9 copy-start.3
  151.5 1.4 copy-start.4
  159.2 69.3 %copy-start.8 = (bf16[256,2560]{1,0:T(8,128)(2,1)S(1)}, bf16[256,2560]{1,0:T(8,128)(2,1)}, u32[]{:S(2)}) copy-start(bf16[256,2560]{1,0:T(8,128)(2,1)} %copy-done.7) | copy-start | bytes 3932164
  159.2 69.3 %copy-start.10 = (bf16[256,2560]{1,0:T(8,128)(2,1)S(1)}, bf16[256,2560]{1,0:T(8,128)(2,1)}, u32[]{:S(2)}) copy-start(bf16[256,2560]{1,0:T(8,128)(2,1)} %copy-done.9) | copy-start | bytes 3932164
Sparse Core Ops, SparseCore 0:
  9.5 40.3 all-gather.6
  52.0 53.9 all-gather.4

commit v3 on v2

--- a/solution.py
+++ b/solution.py
@@ -86,7 +86,7 @@
     )(core, cache, new, queries)
 
 
-def attend_kernel(core_ref, q_own, q_other, kv, w_own, w_other, out, heads):
+def attend_kernel(core_ref, q_own, q_other, kv, heads):
     base = core_ref[0] * TOK
     key_index = iota((4 * TOK, KEYS), 1)
     within = key_index & 127
@@ -110,22 +110,36 @@
         mixed = (f32_dot(probs.astype(jnp.bfloat16), values) / denom).astype(jnp.bfloat16)
         for h in range(4):
             heads[rows, h * HEAD_WIDTH : (h + 1) * HEAD_WIDTH] = mixed[h * TOK : (h + 1) * TOK]
+
+
+def attend(core, q_own, q_other, kv):
+    return pl.pallas_call(
+        attend_kernel,
+        out_shape=jax.ShapeDtypeStruct((4 * TOK, 512), jnp.bfloat16),
+        in_specs=[pl.BlockSpec(memory_space=pltpu.SMEM)] + whole(3),
+        out_specs=whole(1)[0],
+        compiler_params=pltpu.CompilerParams(vmem_limit_bytes=32 * MIB),
+        cost_estimate=pl.CostEstimate(flops=4 * 10**9, bytes_accessed=8 * MIB, transcendentals=MIB),
+        name="attend",
+    )(core, q_own, q_other, kv)
+
+
+def project_kernel(heads, w_own, w_other, out):
     out[...] = (f32_dot(heads[:, :256], w_own[...]) + f32_dot(heads[:, 256:], w_other[...])).astype(
         jnp.bfloat16
     )
 
 
-def attend(core, q_own, q_other, kv, w_own, w_other):
-    return pl.pallas_call(
-        attend_kernel,
+def project(heads, w_own, w_other):
+    return pl.pallas_call(
+        project_kernel,
         out_shape=jax.ShapeDtypeStruct((4 * TOK, D), jnp.bfloat16),
-        in_specs=[pl.BlockSpec(memory_space=pltpu.SMEM)] + whole(5),
+        in_specs=whole(3),
         out_specs=whole(1)[0],
-        scratch_shapes=[pltpu.VMEM((4 * TOK, 512), jnp.bfloat16)],
-        compiler_params=pltpu.CompilerParams(vmem_limit_bytes=32 * MIB),
-        cost_estimate=pl.CostEstimate(flops=10**9, bytes_accessed=4 * MIB, transcendentals=MIB),
-        name="attend",
-    )(core, q_own, q_other, kv, w_own, w_other)
+        compiler_params=pltpu.CompilerParams(vmem_limit_bytes=16 * MIB),
+        cost_estimate=pl.CostEstimate(flops=10**9, bytes_accessed=4 * MIB, transcendentals=0),
+        name="project",
+    )(heads, w_own, w_other)
 
 
 def routing_kernel(routes, weights, select, combine_hi, combine_lo):
@@ -322,7 +336,7 @@
     select, combine_hi, combine_lo = routing(routes[0], gate_weights[0])
     full_gate_up = lax.all_gather(gate_up[0], CTX, axis=0, tiled=True)
     full_down = lax.all_gather(down_proj[0], CTX, axis=0, tiled=True)
-    partial = attend(core.reshape(1), q_own, q_other, kv, out_weight, w_other)
+    partial = project(attend(core.reshape(1), q_own, q_other, kv), out_weight, w_other)
     shares = lax.all_to_all(partial.reshape(4, TOK, D), "yh", 0, 0, tiled=True).reshape(4 * TOK, D)
     rows, residual = pack(shares, hidden[0], norm_gain.reshape(1, D), select)
     arrived = lax.all_to_all(rows.reshape(EXPERTS, BLOCK, WIDTH), EXP, 0, 0, tiled=True)

time: 238 us -> 239 us (level)
  blocking collectives: 71.5 us -> 74.4 us
    all_to_all x1, blocking collectives: 69.2 us -> 72.1 us  [on_device(): lax.all_to_all(outputs.reshape(EXPERTS, BLOCK, WIDTH), EXP, 0, 0, tiled=T...]
where the time goes in v3:
time: 239 us
  waiting for transfers between devices  96.4 us (40%)
  blocking collectives  74.4 us (31%)
  starting transfers between devices  28.7 us (12%)
  Pallas kernels  17.8 us (7%)
  between operations  13.6 us (6%)
  local copies, waits for them, and re-layouts  8.1 us (3%)
    all_to_all x1, blocking collectives, on_device(): lax.all_to_all(outputs.reshape(EXPERTS, BLOCK, WIDTH), EXP, 0, 0, tiled=T...  72.1 us
    all_to_all x1, waiting for transfers between devices, on_device(): lax.all_to_all(rows.reshape(EXPERTS, BLOCK, WIDTH), EXP, 0, 0, tiled=True)  42.7 us
    all_to_all x1, waiting for transfers between devices, on_device(): lax.all_to_all(partial.reshape(4, TOK, D), 'yh', 0, 0, tiled=True)  23.5 us
    all_gather x1, waiting for transfers between devices, on_device(): full_gate_up = lax.all_gather(gate_up[0], CTX, axis=0, tiled=True)  19.8 us
    all_to_all x1, starting transfers between devices, on_device(): lax.all_to_all(rows.reshape(EXPERTS, BLOCK, WIDTH), EXP, 0, 0, tiled=True)  14.8 us
    all_to_all x1, waiting for transfers between devices, on_device(): kv = lax.all_to_all(kv_send, 'yh', 0, 0, tiled=True).reshape(KEYS // 2, 256)  9.01 us
    unnamed x28, local copies, waits for them, and re-layouts  8.1 us
    pallas_call x1, Pallas kernels, experts(): pl.pallas_call(experts_kernel, out_shape=jax.ShapeDtypeStruct((ROWS, WIDT...  6.22 us
  transfers between devices with their start and end apart: 7, of which 4 were waited for; matrix products, arithmetic and copies ran while one was open for 0% of the time, Pallas kernels for 4%

profile of v3, /device:TPU:8, one launch (start us, length us, event | category | flops | bytes accessed | tf_op | source)
XLA Modules:
  0.0 238.9 jit_solution(12661446215021523156)
XLA Ops:
  6.5 0.0 all-gather.7.cloned.1.call-start
  6.5 0.7 all-gather.7.cloned.1.call-update
  7.3 1.9 collective-permute-start.1
  9.2 1.8 prepare.1
  11.0 6.2 %all-to-all-start = ((bf16[4,128,256]{2,1,0:T(8,128)(2,1)}), bf16[4,128,256]{2,1,0:T(8,128)(2,1)S(1)}, u32[]{:S(2)}, u32[]{:S(2)}) async-start(bf16[4,128,256]{2,1,0:T(8,128)(2,1)} %get-tuple-element.15), calls=%async_computation | async-start | bytes 524288 | tf_op jit(solution)/shard_map/all_to_all | solution.py:332
  17.2 2.1 collective-permute-start
  19.4 9.0 %all-to-all-done = bf16[4,128,256]{2,1,0:T(8,128)(2,1)S(1)} async-done(((bf16[4,128,256]{2,1,0:T(8,128)(2,1)}), bf16[4,128,256]{2,1,0:T(8,128)(2,1)S(1)}, u32[]{:S(2)}, u32[]{:S(2)}) %all-to-all-start) | async-done | bytes 262176 | tf_op jit(solution)/shard_map/all_to_all | solution.py:332
  28.4 2.2 all_gather.9.kv
  30.6 0.0 collective-permute-done.q_other
  30.6 0.0 copy-start.5
  30.6 0.9 copy-done.5
  31.5 0.0 copy-start.3
  31.5 2.2 attend.1.heads
  33.7 0.0 copy-start.11
  33.7 0.0 copy-start.12
  33.7 0.0 collective-permute-done.1.w_other
  33.7 0.0 copy-done.3
  33.7 1.7 project.1
  35.4 0.0 copy-start.4
  35.4 0.0 copy-start.6
  35.4 3.7 %all-to-all-start.1 = ((bf16[4,64,2048]{2,1,0:T(8,128)(2,1)}), bf16[4,64,2048]{2,1,0:T(8,128)(2,1)S(1)}, u32[]{:S(2)}, u32[]{:S(2)}) async-start(bf16[4,64,2048]{2,1,0:T(8,128)(2,1)} %bitcast.5), calls=%async_computation.1 | async-start | bytes 2097152 | tf_op jit(solution)/shard_map/all_to_all | solution.py:340
  39.1 0.0 all-gather.5.cloned.1.call-start
  39.1 0.7 all-gather.5.cloned.1.call-update
  39.8 0.0 copy-done.11
  39.8 0.1 copy.12
  39.9 0.0 copy-done.12
  39.9 0.1 copy.11
  40.0 2.5 %routing.1 = (bf16[2560,256]{1,0:T(8,128)(2,1)S(1)}, bf16[256,2560]{1,0:T(8,128)(2,1)S(1)}, bf16[256,2560]{1,0:T(8,128)(2,1)S(1)}) custom-call(s32[64,8]{1,0:T(8,128)S(1)} %bitcast.24, f32[64,8]{1,0:T(8,128)S(1)} %bitcast.23), custom_call_target="tpu_custom_call" | custom-call | flops 1000000000 | bytes 4194304 | tf_op jit(solution)/shard_map/routing/pallas_call | solution.py:194
  42.5 0.0 copy-start.7
  42.5 1.1 copy-done.7
  43.7 0.0 copy-start.9
  43.7 1.1 copy-done.9
  44.7 23.5 %all-to-all-done.1 = bf16[4,64,2048]{2,1,0:T(8,128)(2,1)S(1)} async-done(((bf16[4,64,2048]{2,1,0:T(8,128)(2,1)}), bf16[4,64,2048]{2,1,0:T(8,128)(2,1)S(1)}, u32[]{:S(2)}, u32[]{:S(2)}) %all-to-all-start.1) | async-done | bytes 1048608 | tf_op jit(solution)/shard_map/all_to_all | solution.py:340
  68.2 0.0 copy-done.4
  68.2 0.0 copy-done.6
  68.2 1.1 pack.1
  69.3 0.0 copy-start
  69.4 1.5 copy-done
  70.8 14.8 %all-to-all-start.2 = ((bf16[64,40,512]{2,1,0:T(8,128)(2,1)}), bf16[64,40,512]{2,1,0:T(8,128)(2,1)S(1)}, u32[]{:S(2)}, u32[]{:S(2)}) async-start(bf16[64,40,512]{2,1,0:T(8,128)(2,1)} %bitcast.19), calls=%async_computation.2 | async-start | bytes 5242880 | tf_op jit(solution)/shard_map/all_to_all | solution.py:342
  85.7 0.0 all-gather.7.cloned.1.call-done
  85.7 19.8 %all-gather.5.cloned.1.call-done = bf16[1,2048,768]{2,1,0:T(8,128)(2,1)} async-done(((bf16[1,256,768]{2,1,0:T(8,128)(2,1)}), bf16[1,2048,768]{2,1,0:T(8,128)(2,1)}) %all-gather.5.cloned.1.call-update) | async-done | bytes 3145744 | tf_op jit(solution)/shard_map/all_gather | solution.py:337
  105.5 42.7 %all-to-all-done.2 = bf16[64,40,512]{2,1,0:T(8,128)(2,1)S(1)} async-done(((bf16[64,40,512]{2,1,0:T(8,128)(2,1)}), bf16[64,40,512]{2,1,0:T(8,128)(2,1)S(1)}, u32[]{:S(2)}, u32[]{:S(2)}) %all-to-all-start.2) | async-done | bytes 2621472 | tf_op jit(solution)/shard_map/all_to_all | solution.py:342
  148.2 0.0 copy-start.1
  148.2 1.9 copy-done.1
  150.1 0.0 copy-start.2
  150.1 1.4 copy-done.2
  151.5 6.2 %experts.1 = bf16[2560,512]{1,0:T(8,128)(2,1)S(1)} custom-call(bf16[2560,512]{1,0:T(8,128)(2,1)S(1)} %bitcast.18, bf16[2048,768]{1,0:T(8,128)(2,1)S(1)} %bitcast.25, bf16[2048,384]{1,0:T(8,128)(2,1)S(1)} %bitcast.26), custom_call_target="tpu_custom_call" | custom-call | flops 4000000000 | bytes 10485760 | tf_op jit(solution)/shard_map/experts/pallas_call | solution.py:283
  157.7 0.0 copy-start.8
  157.7 0.0 copy-start.10
  157.7 72.1 %all_to_all.20 = bf16[64,40,512]{2,1,0:T(8,128)(2,1)S(1)} all-to-all(bf16[64,40,512]{2,1,0:T(8,128)(2,1)S(1)} %bitcast.21), channel_id=1, replica_groups=mesh['yh'=4,'core'=2,'x'=4,'z'=8,'yl'=2] {'x','z','yl'}, dimensions={0} | all-to-all | bytes 5242880 | tf_op jit(solution)/shard_map/all_to_all | solution.py:344
  229.9 0.0 copy-done.8
  229.9 0.0 copy-done.10
  229.9 2.2 combine.1
Async XLA Ops:
  6.5 79.1 %all-gather.7.cloned.1.call-start = ((), (), s32[]{:S(2)}) async-start(), calls=%async_computation.5 | async-start | bytes 1769472 | tf_op jit(solution)/shard_map/all_gather | solution.py:338
  7.3 26.5 %collective-permute-start.1 = (bf16[256,2048]{1,0:T(8,128)(2,1)}, bf16[256,2048]{1,0:T(8,128)(2,1)S(1)}, u32[]{:S(2)}, u32[]{:S(2)}) collective-permute-start(bf16[256,2048]{1,0:T(8,128)(2,1)} %w_own.1), channel_id=1, source_target_pairs={{0,64},{64,0},{1,65},{65,1},{2,66},{66,2},{3,67},{67,3},{4,68},{68... | collective-permute-start | bytes 3145736 | tf_op jit(solution)/shard_map/ppermute | solution.py:335
  11.0 17.3 %all-to-all-start = ((bf16[4,128,256]{2,1,0:T(8,128)(2,1)}), bf16[4,128,256]{2,1,0:T(8,128)(2,1)S(1)}, u32[]{:S(2)}, u32[]{:S(2)}) async-start(bf16[4,128,256]{2,1,0:T(8,128)(2,1)} %get-tuple-element.15), calls=%async_computation | async-start | bytes 524288 | tf_op jit(solution)/shard_map/all_to_all | solution.py:332
  17.2 13.4 %collective-permute-start = (bf16[256,256]{1,0:T(8,128)(2,1)}, bf16[256,256]{1,0:T(8,128)(2,1)S(1)}, u32[]{:S(2)}, u32[]{:S(2)}) collective-permute-start(bf16[256,256]{1,0:T(8,128)(2,1)} %get-tuple-element.14), channel_id=1, source_target_pairs={{0,64},{64,0},{1,65},{65,1},{2,66},{66,2},{3,67},{67,3},{4,68},{68... | collective-permute-start | bytes 393224 | tf_op jit(solution)/shard_map/ppermute | solution.py:334
  30.6 0.9 copy-start.5
  31.5 2.2 copy-start.3
  33.7 6.1 %copy-start.11 = (f32[1,64,8]{1,2,0:T(8,128)S(1)}, f32[1,64,8]{1,2,0:T(8,128)}, u32[]{:S(2)}) copy-start(f32[1,64,8]{1,2,0:T(8,128)} %param.17) | copy-start | bytes 6148
  33.7 6.2 %copy-start.12 = (s32[1,64,8]{1,2,0:T(8,128)S(1)}, s32[1,64,8]{1,2,0:T(8,128)}, u32[]{:S(2)}) copy-start(s32[1,64,8]{1,2,0:T(8,128)} %param.16) | copy-start | bytes 6148
  35.4 32.8 %copy-start.4 = (bf16[1,64,2048]{2,1,0:T(8,128)(2,1)S(1)}, bf16[1,64,2048]{2,1,0:T(8,128)(2,1)}, u32[]{:S(2)}) copy-start(bf16[1,64,2048]{2,1,0:T(8,128)(2,1)} %param.13) | copy-start | bytes 786436
  35.4 32.8 %copy-start.6 = (f32[2048]{0:T(1024)S(1)}, f32[2048]{0:T(1024)}, u32[]{:S(2)}) copy-start(f32[2048]{0:T(1024)} %param.15) | copy-start | bytes 24580
  35.4 32.8 %all-to-all-start.1 = ((bf16[4,64,2048]{2,1,0:T(8,128)(2,1)}), bf16[4,64,2048]{2,1,0:T(8,128)(2,1)S(1)}, u32[]{:S(2)}, u32[]{:S(2)}) async-start(bf16[4,64,2048]{2,1,0:T(8,128)(2,1)} %bitcast.5), calls=%async_computation.1 | async-start | bytes 2097152 | tf_op jit(solution)/shard_map/all_to_all | solution.py:340
  39.1 66.4 %all-gather.5.cloned.1.call-start = ((), (), s32[]{:S(2)}) async-start(), calls=%async_computation.4 | async-start | bytes 3538944 | tf_op jit(solution)/shard_map/all_gather | solution.py:337
  42.5 1.2 copy-start.7
  43.7 1.1 copy-start.9
  69.3 1.5 copy-start
  70.8 77.3 %all-to-all-start.2 = ((bf16[64,40,512]{2,1,0:T(8,128)(2,1)}), bf16[64,40,512]{2,1,0:T(8,128)(2,1)S(1)}, u32[]{:S(2)}, u32[]{:S(2)}) async-start(bf16[64,40,512]{2,1,0:T(8,128)(2,1)} %bitcast.19), calls=%async_computation.2 | async-start | bytes 5242880 | tf_op jit(solution)/shard_map/all_to_all | solution.py:342
  148.2 1.9 copy-start.1
  150.1 1.4 copy-start.2
  157.7 72.2 %copy-start.8 = (bf16[256,2560]{1,0:T(8,128)(2,1)S(1)}, bf16[256,2560]{1,0:T(8,128)(2,1)}, u32[]{:S(2)}) copy-start(bf16[256,2560]{1,0:T(8,128)(2,1)} %copy-done.7) | copy-start | bytes 3932164
  157.7 72.2 %copy-start.10 = (bf16[256,2560]{1,0:T(8,128)(2,1)S(1)}, bf16[256,2560]{1,0:T(8,128)(2,1)}, u32[]{:S(2)}) copy-start(bf16[256,2560]{1,0:T(8,128)(2,1)} %copy-done.9) | copy-start | bytes 3932164
Sparse Core Ops, SparseCore 0:
  9.5 40.9 all-gather.6
  52.6 52.8 all-gather.4

commit v4 on v3

--- a/solution.py
+++ b/solution.py
@@ -295,6 +295,33 @@
     )(rows, gate_up, down)
 
 
+def stage_kernel(gate_up, down, up_out, down_out, arrivals):
+    fetches = [
+        pltpu.make_async_copy(gate_up, up_out, arrivals.at[0]),
+        pltpu.make_async_copy(down, down_out, arrivals.at[1]),
+    ]
+    for fetch in fetches:
+        fetch.start()
+    for fetch in fetches:
+        fetch.wait()
+
+
+def stage(gate_up, down):
+    return pl.pallas_call(
+        stage_kernel,
+        out_shape=[
+            jax.ShapeDtypeStruct((D, 2 * FF), jnp.bfloat16),
+            jax.ShapeDtypeStruct((D, FF), jnp.bfloat16),
+        ],
+        in_specs=[pl.BlockSpec(memory_space=pl.ANY)] * 2,
+        out_specs=whole(2),
+        scratch_shapes=[pltpu.SemaphoreType.DMA((2,))],
+        compiler_params=pltpu.CompilerParams(vmem_limit_bytes=46 * MIB),
+        cost_estimate=pl.CostEstimate(flops=0, bytes_accessed=9 * MIB, transcendentals=0),
+        name="stage",
+    )(gate_up, down)
+
+
 def combine_kernel(results, residual, combine_hi, combine_lo, out):
     total = f32_dot(combine_hi[...], results[...]) + f32_dot(combine_lo[...], results[...])
     for part in range(PARTS):
@@ -340,6 +367,7 @@
     shares = lax.all_to_all(partial.reshape(4, TOK, D), "yh", 0, 0, tiled=True).reshape(4 * TOK, D)
     rows, residual = pack(shares, hidden[0], norm_gain.reshape(1, D), select)
     arrived = lax.all_to_all(rows.reshape(EXPERTS, BLOCK, WIDTH), EXP, 0, 0, tiled=True)
+    full_gate_up, full_down = stage(full_gate_up, full_down)
     outputs = experts(arrived.reshape(ROWS, WIDTH), full_gate_up, full_down)
     results = lax.all_to_all(outputs.reshape(EXPERTS, BLOCK, WIDTH), EXP, 0, 0, tiled=True)
     return combine(results.reshape(ROWS, WIDTH), residual, combine_hi, combine_lo)[None]

time: 239 us -> 237 us (level)
  waiting for transfers between devices: 96.4 us -> 90.4 us
  local copies, waits for them, and re-layouts: 8.1 us -> 12.3 us
  blocking collectives: 74.4 us -> 71.3 us
    all_to_all x1, waiting for transfers between devices: 42.7 us -> 37.1 us  [on_device(): lax.all_to_all(rows.reshape(EXPERTS, BLOCK, WIDTH), EXP, 0, 0, tiled=True)]
    unnamed x28 -> x34, local copies, waits for them, and re-layouts: 8.1 us -> 12.3 us
    all_to_all x1, blocking collectives: 72.1 us -> 69 us  [on_device(): lax.all_to_all(outputs.reshape(EXPERTS, BLOCK, WIDTH), EXP, 0, 0, tiled=T...]
  transfers between devices with their start and end apart: 7 -> 7, of which waited for: 4 -> 4; matrix products, arithmetic and copies ran while one was open for 0% -> 0% of each run, Pallas kernels for 4% -> 5%
where the time goes in v4:
time: 237 us; the launch traced here: 236 us
  waiting for transfers between devices  90.4 us (38%)
  blocking collectives  71.3 us (30%)
  starting transfers between devices  28.8 us (12%)
  Pallas kernels  19.7 us (8%)
  between operations  13.6 us (6%)
  local copies, waits for them, and re-layouts  12.3 us (5%)
    all_to_all x1, blocking collectives, on_device(): lax.all_to_all(outputs.reshape(EXPERTS, BLOCK, WIDTH), EXP, 0, 0, tiled=T...  69 us
    all_to_all x1, waiting for transfers between devices, on_device(): lax.all_to_all(rows.reshape(EXPERTS, BLOCK, WIDTH), EXP, 0, 0, tiled=True)  37.1 us
    all_to_all x1, waiting for transfers between devices, on_device(): lax.all_to_all(partial.reshape(4, TOK, D), 'yh', 0, 0, tiled=True)  23.5 us
    all_gather x1, waiting for transfers between devices, on_device(): full_gate_up = lax.all_gather(gate_up[0], CTX, axis=0, tiled=True)  19.4 us
    all_to_all x1, starting transfers between devices, on_device(): lax.all_to_all(rows.reshape(EXPERTS, BLOCK, WIDTH), EXP, 0, 0, tiled=True)  14.8 us
    unnamed x34, local copies, waits for them, and re-layouts  12.3 us
    all_to_all x1, waiting for transfers between devices, on_device(): kv = lax.all_to_all(kv_send, 'yh', 0, 0, tiled=True).reshape(KEYS // 2, 256)  9.01 us
    all_to_all x1, starting transfers between devices, on_device(): kv = lax.all_to_all(kv_send, 'yh', 0, 0, tiled=True).reshape(KEYS // 2, 256)  6.21 us
  transfers between devices with their start and end apart: 7, of which 4 were waited for; matrix products, arithmetic and copies ran while one was open for 0% of the time, Pallas kernels for 5%

profile of v4, /device:TPU:8, one launch (start us, length us, event | category | flops | bytes accessed | tf_op | source)
XLA Modules:
  0.0 235.9 jit_solution(13156228202782911333)
XLA Ops:
  6.5 0.0 all-gather.7.cloned.1.call-start
  6.5 0.7 all-gather.7.cloned.1.call-update
  7.3 1.9 collective-permute-start.1
  9.2 1.8 prepare.1
  11.0 6.2 %all-to-all-start = ((bf16[4,128,256]{2,1,0:T(8,128)(2,1)}), bf16[4,128,256]{2,1,0:T(8,128)(2,1)S(1)}, u32[]{:S(2)}, u32[]{:S(2)}) async-start(bf16[4,128,256]{2,1,0:T(8,128)(2,1)} %get-tuple-element.17), calls=%async_computation | async-start | bytes 524288 | tf_op jit(solution)/shard_map/all_to_all | solution.py:359
  17.2 2.1 collective-permute-start
  19.4 9.0 %all-to-all-done = bf16[4,128,256]{2,1,0:T(8,128)(2,1)S(1)} async-done(((bf16[4,128,256]{2,1,0:T(8,128)(2,1)}), bf16[4,128,256]{2,1,0:T(8,128)(2,1)S(1)}, u32[]{:S(2)}, u32[]{:S(2)}) %all-to-all-start) | async-done | bytes 262176 | tf_op jit(solution)/shard_map/all_to_all | solution.py:359
  28.4 2.2 all_gather.9.kv
  30.6 0.0 collective-permute-done.q_other
  30.6 0.0 copy-start.8
  30.6 0.9 copy-done.8
  31.5 0.0 copy-start.6
  31.5 2.2 attend.1.heads
  33.7 0.0 copy-start.14
  33.7 0.0 copy-start.15
  33.7 0.0 collective-permute-done.1.w_other
  33.7 0.0 copy-done.6
  33.7 1.7 project.1
  35.4 0.0 copy-start.7
  35.4 0.0 copy-start.9
  35.4 3.7 %all-to-all-start.1 = ((bf16[4,64,2048]{2,1,0:T(8,128)(2,1)}), bf16[4,64,2048]{2,1,0:T(8,128)(2,1)S(1)}, u32[]{:S(2)}, u32[]{:S(2)}) async-start(bf16[4,64,2048]{2,1,0:T(8,128)(2,1)} %bitcast.5), calls=%async_computation.1 | async-start | bytes 2097152 | tf_op jit(solution)/shard_map/all_to_all | solution.py:367
  39.1 0.0 all-gather.5.cloned.1.call-start
  39.1 0.7 all-gather.5.cloned.1.call-update
  39.8 0.0 copy-done.14
  39.9 0.1 copy.11
  39.9 0.0 copy-done.15
  39.9 0.1 copy.12
  40.0 2.5 %routing.1 = (bf16[2560,256]{1,0:T(8,128)(2,1)S(1)}, bf16[256,2560]{1,0:T(8,128)(2,1)S(1)}, bf16[256,2560]{1,0:T(8,128)(2,1)S(1)}) custom-call(s32[64,8]{1,0:T(8,128)S(1)} %bitcast.24, f32[64,8]{1,0:T(8,128)S(1)} %bitcast.25), custom_call_target="tpu_custom_call" | custom-call | flops 1000000000 | bytes 4194304 | tf_op jit(solution)/shard_map/routing/pallas_call | solution.py:194
  42.5 0.0 copy-start.10
  42.5 1.1 copy-done.10
  43.7 0.0 copy-start.12
  43.7 1.0 copy-done.12
  44.7 23.5 %all-to-all-done.1 = bf16[4,64,2048]{2,1,0:T(8,128)(2,1)S(1)} async-done(((bf16[4,64,2048]{2,1,0:T(8,128)(2,1)}), bf16[4,64,2048]{2,1,0:T(8,128)(2,1)S(1)}, u32[]{:S(2)}, u32[]{:S(2)}) %all-to-all-start.1) | async-done | bytes 1048608 | tf_op jit(solution)/shard_map/all_to_all | solution.py:367
  68.2 0.0 copy-done.7
  68.2 0.0 copy-done.9
  68.2 1.1 pack.1
  69.3 0.0 copy-start
  69.3 1.5 copy-done
  70.8 14.8 %all-to-all-start.2 = ((bf16[64,40,512]{2,1,0:T(8,128)(2,1)}), bf16[64,40,512]{2,1,0:T(8,128)(2,1)S(1)}, u32[]{:S(2)}, u32[]{:S(2)}) async-start(bf16[64,40,512]{2,1,0:T(8,128)(2,1)} %bitcast.19), calls=%async_computation.2 | async-start | bytes 5242880 | tf_op jit(solution)/shard_map/all_to_all | solution.py:369
  85.7 0.0 all-gather.7.cloned.1.call-done
  85.7 19.4 %all-gather.5.cloned.1.call-done = bf16[1,2048,768]{2,1,0:T(8,128)(2,1)} async-done(((bf16[1,256,768]{2,1,0:T(8,128)(2,1)}), bf16[1,2048,768]{2,1,0:T(8,128)(2,1)}) %all-gather.5.cloned.1.call-update) | async-done | bytes 3145744 | tf_op jit(solution)/shard_map/all_gather | solution.py:364
  105.1 0.0 copy-start.1
  105.1 1.4 copy-done.1
  106.5 1.9 stage.1
  108.4 0.0 copy-start.2
  108.5 1.6 copy-done.2
  110.1 0.0 copy-start.4
  110.1 1.1 copy-done.4
  111.2 37.1 %all-to-all-done.2 = bf16[64,40,512]{2,1,0:T(8,128)(2,1)S(1)} async-done(((bf16[64,40,512]{2,1,0:T(8,128)(2,1)}), bf16[64,40,512]{2,1,0:T(8,128)(2,1)S(1)}, u32[]{:S(2)}, u32[]{:S(2)}) %all-to-all-start.2) | async-done | bytes 2621472 | tf_op jit(solution)/shard_map/all_to_all | solution.py:369
  148.3 0.0 copy-start.3
  148.3 1.9 copy-done.3
  150.2 0.0 copy-start.5
  150.2 1.4 copy-done.5
  151.6 6.2 %experts.1 = bf16[2560,512]{1,0:T(8,128)(2,1)S(1)} custom-call(bf16[2560,512]{1,0:T(8,128)(2,1)S(1)} %bitcast.18, bf16[2048,768]{1,0:T(8,128)(2,1)S(1)} %copy-done.3, bf16[2048,384]{1,0:T(8,128)(2,1)S(1)} %copy-done.5), custom_call_target="tpu_custom_call" | custom-call | flops 4000000000 | bytes 10485760 | tf_op jit(solution)/shard_map/experts/pallas_call | solution.py:283
  157.8 0.0 copy-start.11
  157.8 0.0 copy-start.13
  157.8 69.0 %all_to_all.20 = bf16[64,40,512]{2,1,0:T(8,128)(2,1)S(1)} all-to-all(bf16[64,40,512]{2,1,0:T(8,128)(2,1)S(1)} %bitcast.21), channel_id=1, replica_groups=mesh['yh'=4,'core'=2,'x'=4,'z'=8,'yl'=2] {'x','z','yl'}, dimensions={0} | all-to-all | bytes 5242880 | tf_op jit(solution)/shard_map/all_to_all | solution.py:372
  226.9 0.0 copy-done.11
  226.9 0.0 copy-done.13
  226.9 2.2 combine.1
Async XLA Ops:
  6.5 79.1 %all-gather.7.cloned.1.call-start = ((), (), s32[]{:S(2)}) async-start(), calls=%async_computation.5 | async-start | bytes 1769472 | tf_op jit(solution)/shard_map/all_gather | solution.py:365
  7.3 26.5 %collective-permute-start.1 = (bf16[256,2048]{1,0:T(8,128)(2,1)}, bf16[256,2048]{1,0:T(8,128)(2,1)S(1)}, u32[]{:S(2)}, u32[]{:S(2)}) collective-permute-start(bf16[256,2048]{1,0:T(8,128)(2,1)} %w_own.1), channel_id=1, source_target_pairs={{0,64},{64,0},{1,65},{65,1},{2,66},{66,2},{3,67},{67,3},{4,68},{68... | collective-permute-start | bytes 3145736 | tf_op jit(solution)/shard_map/ppermute | solution.py:362
  11.0 17.3 %all-to-all-start = ((bf16[4,128,256]{2,1,0:T(8,128)(2,1)}), bf16[4,128,256]{2,1,0:T(8,128)(2,1)S(1)}, u32[]{:S(2)}, u32[]{:S(2)}) async-start(bf16[4,128,256]{2,1,0:T(8,128)(2,1)} %get-tuple-element.17), calls=%async_computation | async-start | bytes 524288 | tf_op jit(solution)/shard_map/all_to_all | solution.py:359
  17.2 13.4 %collective-permute-start = (bf16[256,256]{1,0:T(8,128)(2,1)}, bf16[256,256]{1,0:T(8,128)(2,1)S(1)}, u32[]{:S(2)}, u32[]{:S(2)}) collective-permute-start(bf16[256,256]{1,0:T(8,128)(2,1)} %get-tuple-element.16), channel_id=1, source_target_pairs={{0,64},{64,0},{1,65},{65,1},{2,66},{66,2},{3,67},{67,3},{4,68},{68... | collective-permute-start | bytes 393224 | tf_op jit(solution)/shard_map/ppermute | solution.py:361
  30.6 0.9 copy-start.8
  31.5 2.2 copy-start.6
  33.7 6.1 %copy-start.14 = (s32[1,64,8]{1,2,0:T(8,128)S(1)}, s32[1,64,8]{1,2,0:T(8,128)}, u32[]{:S(2)}) copy-start(s32[1,64,8]{1,2,0:T(8,128)} %param.16) | copy-start | bytes 6148
  33.7 6.2 %copy-start.15 = (f32[1,64,8]{1,2,0:T(8,128)S(1)}, f32[1,64,8]{1,2,0:T(8,128)}, u32[]{:S(2)}) copy-start(f32[1,64,8]{1,2,0:T(8,128)} %param.17) | copy-start | bytes 6148
  35.4 32.8 %copy-start.7 = (bf16[1,64,2048]{2,1,0:T(8,128)(2,1)S(1)}, bf16[1,64,2048]{2,1,0:T(8,128)(2,1)}, u32[]{:S(2)}) copy-start(bf16[1,64,2048]{2,1,0:T(8,128)(2,1)} %param.13) | copy-start | bytes 786436
  35.4 32.8 %copy-start.9 = (f32[2048]{0:T(1024)S(1)}, f32[2048]{0:T(1024)}, u32[]{:S(2)}) copy-start(f32[2048]{0:T(1024)} %param.15) | copy-start | bytes 24580
  35.4 32.8 %all-to-all-start.1 = ((bf16[4,64,2048]{2,1,0:T(8,128)(2,1)}), bf16[4,64,2048]{2,1,0:T(8,128)(2,1)S(1)}, u32[]{:S(2)}, u32[]{:S(2)}) async-start(bf16[4,64,2048]{2,1,0:T(8,128)(2,1)} %bitcast.5), calls=%async_computation.1 | async-start | bytes 2097152 | tf_op jit(solution)/shard_map/all_to_all | solution.py:367
  39.1 66.0 %all-gather.5.cloned.1.call-start = ((), (), s32[]{:S(2)}) async-start(), calls=%async_computation.4 | async-start | bytes 3538944 | tf_op jit(solution)/shard_map/all_gather | solution.py:364
  42.5 1.2 copy-start.10
  43.7 1.0 copy-start.12
  69.3 1.5 copy-start
  70.8 77.5 %all-to-all-start.2 = ((bf16[64,40,512]{2,1,0:T(8,128)(2,1)}), bf16[64,40,512]{2,1,0:T(8,128)(2,1)S(1)}, u32[]{:S(2)}, u32[]{:S(2)}) async-start(bf16[64,40,512]{2,1,0:T(8,128)(2,1)} %bitcast.19), calls=%async_computation.2 | async-start | bytes 5242880 | tf_op jit(solution)/shard_map/all_to_all | solution.py:369
  105.1 1.4 copy-start.1
  108.4 1.6 copy-start.2
  110.1 1.2 copy-start.4
  148.3 1.9 copy-start.3
  150.2 1.4 copy-start.5
  157.8 69.1 %copy-start.11 = (bf16[256,2560]{1,0:T(8,128)(2,1)S(1)}, bf16[256,2560]{1,0:T(8,128)(2,1)}, u32[]{:S(2)}) copy-start(bf16[256,2560]{1,0:T(8,128)(2,1)} %copy-done.10) | copy-start | bytes 3932164
  157.8 69.0 %copy-start.13 = (bf16[256,2560]{1,0:T(8,128)(2,1)S(1)}, bf16[256,2560]{1,0:T(8,128)(2,1)}, u32[]{:S(2)}) copy-start(bf16[256,2560]{1,0:T(8,128)(2,1)} %copy-done.12) | copy-start | bytes 3932164
Sparse Core Ops, SparseCore 0:
  9.5 41.0 all-gather.6
  52.7 52.4 all-gather.4
